TPU v7x, 512 devices: a whole 4x4x16 slice. The times are simulated.
512 devices in a mesh: group: 16 (over x, z_hi, core), seq: 32 (over z_lo, y).
Axes of the slice: x: 4, y: 4, z: 16 (z_hi: 2, z_lo: 8; z = z_hi * 8 + z_lo), core: 2. Of those that a mesh axis runs over, the one named last changes fastest.
Arguments:
- queries: bfloat16 [4, 32, 8192], P(None, 'group', 'seq'), may hold values from -128 to 128
- key_value_pages: bfloat16 [16, 512, 32, 2048], P('group', 'seq'), may hold values from -6 to 6
- key_value_scales: bfloat16 [16, 512, 16], P('group', 'seq'), may hold values from 0.5 to 2
- page_table: int32 [16, 32, 16], P('group', 'seq'), may hold values from 0 to 15, each once within a row
- context_len: int32 [32], P('group'), may hold values from 4 to 8192, as said below
- mig_dest: int32 [32, 256], P('group', 'seq'), may hold values from 0 to 15, as said below
Outputs:
- attended: bfloat16 [4, 32, 8192], P(None, 'group', 'seq')
- incoming_pages: bfloat16 [16, 512, 32, 2048], P('group', 'seq')
- incoming_scales: bfloat16 [16, 512, 16], P('group', 'seq')
Inputs may be any that keep to these rules, and one draw needn't show every extreme that they name: `page_table`: each device's 16 entries name its pool slots, each once; slot q of a group uses entries q * 8 to (q + 1) * 8 - 1 for its local pages in order. `context_len`: the cached tokens of a request, the 4 newest included. `mig_dest`: entry s * 8 + j of request r names the group that receives the request's local page j on seq index s, or its home group r // 2 where the page stays. On each seq index a group sends at most one page to each other group.
All inputs are finite; a program needn't handle non-finite values.
Results may differ from a plain program's by a relative error of at most 0.0075.
Values may be sent and summed in bfloat16 or wider, within the bound.
A program may use at most 64 MiB of HBM per device.

v0:
```python
import jax
import jax.numpy as jnp
from jax import lax
from jax.sharding import PartitionSpec as P

NEGATIVE = -1e30


def combined_all(value, axis, join):
    pieces = jax.tree.map(lambda part: lax.all_gather(part, axis), value)
    head = jax.tree.map(lambda part: part[0], pieces)
    tail = jax.tree.map(lambda part: part[1:], pieces)
    subtotal, _ = lax.scan(lambda subtotal, section: (join(subtotal, section), None), head, tail)
    return subtotal


def batched_partial(query_rows, blocks, page_scales, positions, limits, keeping, heads_kv):
    row_count, page_count, page_size, width = blocks.shape
    head_dim = width // (2 * heads_kv)
    step_count = query_rows.shape[1]
    key_rows = blocks[..., : heads_kv * head_dim].reshape(
        row_count, page_count, page_size, heads_kv, head_dim
    )
    value_rows = blocks[..., heads_kv * head_dim :].reshape(
        row_count, page_count, page_size, heads_kv, head_dim
    )
    grouped_query = query_rows.reshape(row_count, step_count, heads_kv, -1, head_dim)
    raw_score = jnp.einsum(
        "rtkgd,rpskd->rtkgps", grouped_query, key_rows, preferred_element_type=jnp.float32
    )
    factors = page_scales.astype(jnp.float32)
    key_factor = factors[..., :heads_kv].transpose(0, 2, 1)[:, None, :, None, :, None]
    value_factor = factors[..., heads_kv:].transpose(0, 2, 1)[:, None, :, None, :, None]
    scores = raw_score * key_factor * head_dim ** (-0.5)
    visible = (positions[:, None, :, :] < limits[:, :, None, None]) & keeping[:, None, :, None]
    visible = visible[:, :, None, None, :, :]
    highest = jnp.max(jnp.where(visible, scores, NEGATIVE), axis=(4, 5))
    exponent_terms = jnp.where(visible, jnp.exp(scores - highest[..., None, None]), 0.0)
    totals = jnp.sum(exponent_terms, axis=(4, 5))
    weights = (exponent_terms * value_factor).astype(jnp.bfloat16)
    context = jnp.einsum(
        "rtkgps,rpskd->rtkgd", weights, value_rows, preferred_element_type=jnp.float32
    )
    head_count = highest.shape[2] * highest.shape[3]
    return (
        highest.reshape(row_count, step_count, head_count),
        totals.reshape(row_count, step_count, head_count),
        context.reshape(row_count, step_count, head_count, head_dim),
    )


def combine_parts(earlier, later):
    highest = jnp.maximum(earlier[0], later[0])
    first_weight = jnp.exp(earlier[0] - highest)
    second_weight = jnp.exp(later[0] - highest)
    return (
        highest,
        earlier[1] * first_weight + later[1] * second_weight,
        earlier[2] * first_weight[..., None] + later[2] * second_weight[..., None],
    )


def local(queries, key_value_pages, key_value_scales, page_table, context_len, mig_dest):
    seq_count = lax.axis_size("seq")
    group_count = lax.axis_size("group")
    seq_index = lax.axis_index("seq")
    group_index = lax.axis_index("group")
    full_query = lax.all_gather(queries, "seq", axis=2, tiled=True)
    step_count, row_count, query_width = full_query.shape
    pool_pages = key_value_pages[0]
    pool_scales = key_value_scales[0]
    pool_size = pool_pages.shape[0]
    page_size = pool_pages.shape[1]
    heads_kv = pool_scales.shape[1] // 2
    head_dim = pool_pages.shape[2] // (2 * heads_kv)
    head_count = query_width // head_dim
    heads_here = head_count // seq_count
    per_row = mig_dest.shape[1]
    slot_table = page_table[0, 0].reshape(row_count, per_row)
    page_number = jnp.arange(per_row, dtype=jnp.int32)[None, :] * seq_count + seq_index
    first_positions = jnp.broadcast_to(page_number * page_size, (row_count, per_row))
    token_offsets = jnp.arange(page_size, dtype=jnp.int32)
    limit_table = (
        context_len[:, None] - step_count + 1 + jnp.arange(step_count, dtype=jnp.int32)[None, :]
    )
    moved = mig_dest != group_index
    group_iota = jnp.arange(group_count, dtype=jnp.int32)
    chosen = (mig_dest[None] == group_iota[:, None, None]) & moved[None]
    slot_onehot = (slot_table[..., None] == jnp.arange(pool_size, dtype=jnp.int32)).astype(
        jnp.bfloat16
    )
    send_select = jnp.einsum(
        "hrj,rjn->hn", chosen.astype(jnp.bfloat16), slot_onehot, preferred_element_type=jnp.float32
    ).astype(jnp.bfloat16)
    send_pages = jnp.einsum(
        "hn,npw->hpw", send_select, pool_pages, preferred_element_type=jnp.float32
    ).astype(jnp.bfloat16)
    send_scales = jnp.dot(send_select, pool_scales, preferred_element_type=jnp.float32).astype(
        jnp.bfloat16
    )
    flat_slots = slot_table.reshape(-1)
    row_blocks = pool_pages[flat_slots].reshape(row_count, per_row, page_size, pool_pages.shape[2])
    row_scale_list = pool_scales[flat_slots].reshape(row_count, per_row, pool_scales.shape[1])
    row_positions = first_positions[..., None] + token_offsets
    query_rows = full_query.transpose(1, 0, 2)
    got_pages, got_scales = (
        lax.all_to_all(send_pages, "group", split_axis=0, concat_axis=0, tiled=True),
        lax.all_to_all(send_scales, "group", split_axis=0, concat_axis=0, tiled=True),
    )
    keep_all = jnp.ones((row_count, per_row), dtype=bool)
    row_parts = batched_partial(
        query_rows, row_blocks, row_scale_list, row_positions, limit_table, keep_all, heads_kv
    )
    merged = combined_all((row_parts[0], row_parts[1], row_parts[2]), "seq", combine_parts)
    own_total = lax.dynamic_slice_in_dim(merged[1], seq_index * heads_here, heads_here, 2)
    own_context = lax.dynamic_slice_in_dim(merged[2], seq_index * heads_here, heads_here, 2)
    output = own_context / own_total[..., None]
    attended = (
        output.transpose(1, 0, 2, 3)
        .reshape(step_count, row_count, heads_here * head_dim)
        .astype(jnp.bfloat16)
    )
    return (attended, got_pages[None], got_scales[None])


def solution(mesh):
    return jax.shard_map(
        local,
        mesh=mesh,
        in_specs=(
            P(None, "group", "seq"),
            P("group", "seq", None, None),
            P("group", "seq", None),
            P("group", "seq", None),
            P("group"),
            P("group", "seq"),
        ),
        out_specs=(P(None, "group", "seq"), P("group", "seq", None, None), P("group", "seq", None)),
        check_vma=False,
    )
```

profile of v0, /device:TPU:12, one launch (start us, length us, event | category | flops | bytes accessed | tf_op | source)
XLA Modules:
  0.0 535.4 jit_solution(5482274705528427389)
XLA Ops:
  8.8 2.0 gather_fusion
  10.8 1.7 fusion.26
  12.5 1.2 copy.71
  14.7 116.0 %all_gather.12 = bf16[4,2,8192]{2,1,0:T(2,128)(2,1)S(1)} all-gather(bf16[4,2,256]{2,1,0:T(2,128)(2,1)S(1)} %copy-done.3), channel_id=1, replica_groups=mesh['group'=16,'seq'=32] {'seq'}, dimensions={2}, use_global_device_ids=true | all-gather | bytes 135168 | tf_op jit(solution)/shard_map/all_gather | solution.py:68
  132.1 1.8 fusion.3
  138.5 14.3 %all-to-all-start.1 = ((bf16[16,1,16]{2,1,0:T(2,128)(2,1)}), bf16[16,1,16]{2,1,0:T(2,128)(2,1)S(1)}, u32[]{:S(2)}, u32[]{:S(2)}) async-start(bf16[16,1,16]{2,1,0:T(2,128)(2,1)} %copy.54), calls=%async_computation.1 | async-start | bytes 16384 | tf_op jit(solution)/shard_map/all_to_all | solution.py:108
  152.8 2.4 convolution_convert_fusion
  155.3 2.5 copy.53
  157.8 8.0 %all-to-all-done.1 = bf16[16,1,16]{2,1,0:T(2,128)(2,1)S(1)} async-done(((bf16[16,1,16]{2,1,0:T(2,128)(2,1)}), bf16[16,1,16]{2,1,0:T(2,128)(2,1)S(1)}, u32[]{:S(2)}, u32[]{:S(2)}) %all-to-all-start.1) | async-done | bytes 544 | tf_op jit(solution)/shard_map/all_to_all | solution.py:108
  165.7 6.5 %all-to-all-start = ((bf16[16,32,2048]{2,1,0:T(8,128)(2,1)}), bf16[16,32,2048]{2,1,0:T(8,128)(2,1)}, u32[]{:S(2)}, u32[]{:S(2)}) async-start(bf16[16,32,2048]{2,1,0:T(8,128)(2,1)} %copy.53), calls=%async_computation | async-start | bytes 4194304 | tf_op jit(solution)/shard_map/all_to_all | solution.py:107
  172.4 181.4 %all_gather.14 = f32[32,2,4,64]{3,2,1,0:T(4,128)S(1)} all-gather(f32[1,2,4,64]{3,2,1,0:T(4,128)S(1)} %all_gather_reshape.10), channel_id=1, replica_groups=mesh['group'=16,'seq'=32] {'seq'}, dimensions={0}, use_global_device_ids=true | all-gather | bytes 67584 | tf_op jit(solution)/shard_map/all_gather | solution.py:10
  353.8 122.0 %all_gather.13 = f32[32,2,4,64]{3,2,1,0:T(4,128)S(1)} all-gather(f32[1,2,4,64]{3,2,1,0:T(4,128)S(1)} %all_gather_reshape.9), channel_id=1, replica_groups=mesh['group'=16,'seq'=32] {'seq'}, dimensions={0}, use_global_device_ids=true | all-gather | bytes 67584 | tf_op jit(solution)/shard_map/all_gather | solution.py:10
  476.5 8.0 %slice.53 = f32[31,2,4,64,128]{4,3,2,1,0:T(8,128)} slice(f32[32,2,4,64,128]{4,3,2,1,0:T(8,128)} %all-gather.2.cloned.1.call-done), slice={[1:32], [0:2], [0:4], [0:64], [0:128]} | slice | bytes 16252928 | tf_op jit(solution)/shard_map/slice | solution.py:12
  485.5 39.1 %while.14 = (s32[]{:T(128)}, f32[2,4,64]{2,1,0:T(4,128)S(1)}, f32[2,4,64]{2,1,0:T(4,128)S(1)}, f32[2,4,64,128]{3,2,1,0:T(8,128)S(1)}, f32[31,2,4,64]{3,2,1,0:T(4...) while((s32[]{:T(128)}, f32[2,4,64]{2,1,0:T(4,128)S(1)}, ...), condition=%wide.region_3.4_spmd, body=%wide.region_2.3_spmd.sunk | while | flops 199682 | bytes 807005 | solution.py:13
  485.5 1.2 fusion.33
  486.8 1.2 fusion.33
  488.1 1.2 fusion.33
  496.9 1.2 fusion.33
  498.1 1.2 fusion.33
  499.4 1.2 fusion.33
  500.7 1.2 fusion.33
  501.9 1.2 fusion.33
  503.2 1.2 fusion.33
  504.5 1.2 fusion.33
  505.7 1.2 fusion.33
  507.0 1.2 fusion.33
  508.2 1.2 fusion.33
  509.5 1.2 fusion.33
  520.9 1.2 fusion.33
  522.1 1.2 fusion.33
  523.4 1.2 fusion.33
  525.4 3.2 copy.105
  (101 shorter events, 28.8 us)
Async XLA Ops:
  7.2 1.6 copy-start
  7.2 469.3 %all-gather.2.cloned.1.call-start = ((), (), s32[]{:S(2)}) async-start(), calls=%async_computation.2 | async-start | bytes 8650752 | tf_op jit(solution)/shard_map/all_gather | solution.py:10
  12.5 1.3 copy-start.2
  12.5 2.1 copy-start.5
  12.5 2.2 copy-start.3
  130.9 1.2 copy-start.1
  135.0 1.8 copy-start.6
  135.0 2.5 copy-start.4
  138.5 27.2 %all-to-all-start.1 = ((bf16[16,1,16]{2,1,0:T(2,128)(2,1)}), bf16[16,1,16]{2,1,0:T(2,128)(2,1)S(1)}, u32[]{:S(2)}, u32[]{:S(2)}) async-start(bf16[16,1,16]{2,1,0:T(2,128)(2,1)} %copy.54), calls=%async_computation.1 | async-start | bytes 16384 | tf_op jit(solution)/shard_map/all_to_all | solution.py:108
  165.7 310.7 %all-to-all-start = ((bf16[16,32,2048]{2,1,0:T(8,128)(2,1)}), bf16[16,32,2048]{2,1,0:T(8,128)(2,1)}, u32[]{:S(2)}, u32[]{:S(2)}) async-start(bf16[16,32,2048]{2,1,0:T(8,128)(2,1)} %copy.53), calls=%async_computation | async-start | bytes 4194304 | tf_op jit(solution)/shard_map/all_to_all | solution.py:107
Sparse Core Ops, SparseCore 0:
  136.4 283.2 all-gather.1
where the time goes:
time: 537 us; the launch traced here: 535 us
  blocking collectives  419 us (78%)
  other arithmetic  41.3 us (8%)
  local copies, waits for them, and re-layouts  25.9 us (5%)
  starting transfers between devices  20.9 us (4%)
  between operations  14.2 us (3%)
  waiting for transfers between devices  8 us (1%)
    all_gather x2, blocking collectives, combined_all(): pieces = jax.tree.map(lambda part: lax.all_gather(part, axis), value)  303 us
    all_gather x1, blocking collectives, local(): full_query = lax.all_gather(queries, 'seq', axis=2, tiled=True)  116 us
    add x31, other arithmetic, combine_parts(): earlier[2] * first_weight[..., None] + later[2] * second_weight[..., None]  37.6 us
    all_to_all x1, starting transfers between devices, local(): lax.all_to_all(send_scales, 'group', split_axis=0, concat_axis=0, tiled=T...  14.3 us
  transfers between devices with their start and end apart: 3, of which 1 were waited for; matrix products, arithmetic and copies ran while one was open for 1% of the time, Pallas kernels for 0%

commit v1 on v0

v1 whole, which is shorter than its diff:
```python
import functools

import jax
import jax.numpy as jnp
from jax import lax
from jax.experimental import pallas as pl
from jax.experimental.pallas import tpu as pltpu
from jax.sharding import PartitionSpec as P

NEGATIVE = -1e30
MESH = pl.DeviceIdType.MESH
NX, NH, NC, NZ, NY = 4, 2, 2, 8, 4
NG = NX * NH * NC
STEPS, RG, PPR, SLOTS, TOKENS = 4, 2, 8, 16, 32
HEADS, DIM = 8, 128
WIDTH = 2 * HEADS * DIM
LOCAL = SLOTS * TOKENS
ROWS = 16


def join(parts):
    context = parts[..., :DIM]
    highest = parts[..., DIM : DIM + 1]
    totals = parts[..., DIM + 1 : DIM + 2]
    top = jnp.max(highest, axis=0)
    factor = jnp.exp(highest - top[None])
    return jnp.sum(context * factor, axis=0), top, jnp.sum(totals * factor, axis=0)


def with_stats(top, total):
    lane = lax.broadcasted_iota(jnp.int32, top.shape[:-1] + (DIM,), top.ndim - 1)
    return jnp.where(lane == 0, top, total)


def kernel(
    table, ctx, mig, query, scales, pages,
    att, out_pages, out_scales,
    pool, send, qall, part, yland, zpart, zland, scale_rows, sc_send, sc_recv,
    pool_sem, own_sem,
    zq_s, zq_r, yq_s, yq_r, pg_s, pg_r, sc_s, sc_r, yr_s, yr_r, zr_s, zr_r,
):
    g = lax.axis_index("group")
    s = lax.axis_index("seq")
    x, zh, c = g // (NH * NC), (g // NC) % NH, g % NC
    zl, y = s // NY, s % NY

    def along_z(d):
        return (g, lax.rem(zl + d, NZ) * NY + y)

    def along_y(d):
        return (g, zl * NY + lax.rem(y + d, NY))

    def along_group(d):
        dx, dc, dz = (d // NC) % NX, d % NC, 1 - d // (NX * NC)
        return (lax.rem(x + dx, NX) * NH + lax.rem(zh + dz, NH)) * NC + lax.rem(c + dc, NC)

    group_steps = [d for d in range(NG) if d != NX * NC]

    load_pool = pltpu.make_async_copy(pages, pool, pool_sem)
    load_pool.start()

    barrier = pltpu.get_barrier_semaphore()
    for d in group_steps:
        pl.semaphore_signal(barrier, 1, device_id=(along_group(d), s), device_id_type=MESH)
    for d in range(1, NZ):
        pl.semaphore_signal(barrier, 1, device_id=along_z(d), device_id_type=MESH)
    for d in range(1, NY):
        pl.semaphore_signal(barrier, 1, device_id=along_y(d), device_id_type=MESH)
    pl.semaphore_wait(barrier, NG - 1 + NZ - 1 + NY - 1)

    z_queries = []
    for d in range(1, NZ):
        copy = pltpu.make_async_remote_copy(
            query, qall.at[y, zl], zq_s.at[d], zq_r.at[d], device_id=along_z(d), device_id_type=MESH
        )
        copy.start()
        z_queries.append(copy)
    qall[y, zl] = query[...]

    load_pool.wait()

    def page_copy(d, h):
        return pltpu.make_async_remote_copy(
            send.at[h], out_pages.at[g], pg_s.at[d], pg_r.at[d], device_id=(h, s), device_id_type=MESH
        )

    def page_for(h):
        found = jnp.int32(0)
        slot = jnp.int32(0)
        for r in range(RG):
            for j in range(PPR):
                here = mig[r, j] == h
                slot = jnp.where(here, table[0, 0, r * PPR + j], slot)
                found = jnp.where(here, 1, found)
        return slot, found

    def send_page(i, carry):
        d = jnp.where(i < NX * NC, i, i + 1)
        h = along_group(d)
        slot, found = page_for(h)
        value = pool[slot]
        send[h] = jnp.where(found > 0, value, jnp.zeros_like(value))
        page_copy(d, h).start()
        return carry

    lax.fori_loop(0, NG - 1, send_page, 0)
    send[g] = jnp.zeros((TOKENS, WIDTH), jnp.bfloat16)
    own_page = pltpu.make_async_copy(send.at[g], out_pages.at[g], own_sem)
    own_page.start()

    slot_iota = lax.broadcasted_iota(jnp.int32, (NG, SLOTS), 1)
    dest_iota = lax.broadcasted_iota(jnp.int32, (NG, SLOTS), 0)
    chosen = jnp.zeros((NG, SLOTS), jnp.float32)
    token = lax.broadcasted_iota(jnp.int32, (8, LOCAL), 1)
    token_slot, token_in = token // TOKENS, token % TOKENS
    position = jnp.zeros((8, LOCAL), jnp.int32)
    owner = jnp.zeros((8, LOCAL), jnp.int32)
    for r in range(RG):
        for j in range(PPR):
            slot = table[0, 0, r * PPR + j]
            dest = mig[r, j]
            chosen = jnp.where(
                (dest_iota == dest) & (slot_iota == slot) & (dest_iota != g), 1.0, chosen
            )
            mine = token_slot == slot
            position = jnp.where(mine, (j * NZ * NY + s) * TOKENS + token_in, position)
            owner = jnp.where(mine, r, owner)
    own_scales = scales[...]
    rows = jnp.dot(chosen.astype(jnp.bfloat16), own_scales, preferred_element_type=jnp.float32)
    rows = jnp.concatenate([rows, jnp.zeros((NG, DIM - 2 * HEADS), jnp.float32)], axis=1)
    for h in range(NG):
        sc_send[h] = rows[h : h + 1]
    sc_recv[g] = jnp.zeros((1, DIM), jnp.float32)
    sc_copies = []
    for d in group_steps:
        h = along_group(d)
        copy = pltpu.make_async_remote_copy(
            sc_send.at[h], sc_recv.at[g], sc_s.at[d], sc_r.at[d], device_id=(h, s), device_id_type=MESH
        )
        copy.start()
        sc_copies.append(copy)

    for copy in z_queries:
        copy.wait()
    y_queries = []
    for d in range(1, NY):
        copy = pltpu.make_async_remote_copy(
            qall.at[y], qall.at[y], yq_s.at[d], yq_r.at[d], device_id=along_y(d), device_id_type=MESH
        )
        copy.start()
        y_queries.append(copy)

    spread = (
        lax.broadcasted_iota(jnp.int32, (SLOTS, LOCAL), 1) // TOKENS
        == lax.broadcasted_iota(jnp.int32, (SLOTS, LOCAL), 0)
    )
    scale_rows[...] = lax.dot_general(
        own_scales, jnp.where(spread, 1.0, 0.0).astype(jnp.bfloat16),
        (((0,), (0,)), ((), ())), preferred_element_type=jnp.float32,
    )
    row = lax.broadcasted_iota(jnp.int32, (NY * ROWS, LOCAL), 0)
    row_request, row_step = (row // 8) % RG, row % STEPS
    limit = jnp.where(row_request == 0, ctx[0], ctx[1]) - STEPS + 1 + row_step
    visible = (position[:1] < limit) & (owner[:1] == row_request)

    for copy in y_queries:
        copy.wait()

    for k in range(HEADS):
        query_rows = qall[:, k].reshape(NY * ROWS, DIM)
        keys = pool[:, :, k * DIM : (k + 1) * DIM].reshape(LOCAL, DIM)
        values = pool[:, :, (HEADS + k) * DIM : (HEADS + k + 1) * DIM].reshape(LOCAL, DIM)
        raw = lax.dot_general(
            query_rows, keys, (((1,), (1,)), ((), ())), preferred_element_type=jnp.float32
        )
        scores = raw * (scale_rows[k : k + 1, :] * DIM**-0.5)
        top = jnp.max(jnp.where(visible, scores, NEGATIVE), axis=1, keepdims=True)
        terms = jnp.where(visible, jnp.exp(scores - top), 0.0)
        total = jnp.sum(terms, axis=1, keepdims=True)
        weights = (terms * scale_rows[HEADS + k : HEADS + k + 1, :]).astype(jnp.bfloat16)
        context = jnp.dot(weights, values, preferred_element_type=jnp.float32)
        part[:, k, :, :DIM] = context.reshape(NY, ROWS, DIM)
        part[:, k, :, DIM:] = with_stats(top, total).reshape(NY, ROWS, DIM)

    y_parts = []
    for d in range(1, NY):
        to = lax.rem(y + d, NY)
        copy = pltpu.make_async_remote_copy(
            part.at[to], yland.at[y], yr_s.at[d], yr_r.at[d], device_id=along_y(d), device_id_type=MESH
        )
        copy.start()
        y_parts.append(copy)
    yland[y] = part[y]
    for copy in y_parts:
        copy.wait()
    for k in range(HEADS):
        context, top, total = join(yland[:, k])
        zpart[k, :, :DIM] = context
        zpart[k, :, DIM:] = with_stats(top, total)

    z_parts = []
    for d in range(1, NZ):
        to = lax.rem(zl + d, NZ)
        copy = pltpu.make_async_remote_copy(
            zpart.at[to], zland.at[zl], zr_s.at[d], zr_r.at[d], device_id=along_z(d), device_id_type=MESH
        )
        copy.start()
        z_parts.append(copy)
    zland[zl] = zpart[zl]
    for copy in z_parts:
        copy.wait()
    context, top, total = join(zland[...])
    att[...] = (context / total).astype(jnp.bfloat16)

    for copy in sc_copies:
        copy.wait()
    for h in range(NG):
        out_scales[h : h + 1, :] = sc_recv[h]

    def wait_page(i, carry):
        d = jnp.where(i < NX * NC, i, i + 1)
        page_copy(d, along_group(d)).wait()
        return carry

    lax.fori_loop(0, NG - 1, wait_page, 0)
    own_page.wait()


def local(queries, key_value_pages, key_value_scales, page_table, context_len, mig_dest):
    query = queries.reshape(STEPS, RG, 2, DIM).transpose(1, 2, 0, 3).reshape(ROWS, DIM)
    dma = pltpu.SemaphoreType.DMA
    vmem = pl.BlockSpec(memory_space=pltpu.VMEM)
    smem = pl.BlockSpec(memory_space=pltpu.SMEM)
    hbm = pl.BlockSpec(memory_space=pl.ANY)
    att, got_pages, got_scales = pl.pallas_call(
        kernel,
        out_shape=(
            jax.ShapeDtypeStruct((ROWS, DIM), jnp.bfloat16),
            jax.ShapeDtypeStruct((NG, TOKENS, WIDTH), jnp.bfloat16),
            jax.ShapeDtypeStruct((NG, DIM), jnp.float32),
        ),
        in_specs=[smem, smem, smem, vmem, vmem, hbm],
        out_specs=(vmem, hbm, vmem),
        scratch_shapes=[
            pltpu.VMEM((SLOTS, TOKENS, WIDTH), jnp.bfloat16),
            pltpu.VMEM((NG, TOKENS, WIDTH), jnp.bfloat16),
            pltpu.VMEM((NY, NZ, ROWS, DIM), jnp.bfloat16),
            pltpu.VMEM((NY, NZ, ROWS, 2 * DIM), jnp.float32),
            pltpu.VMEM((NY, NZ, ROWS, 2 * DIM), jnp.float32),
            pltpu.VMEM((NZ, ROWS, 2 * DIM), jnp.float32),
            pltpu.VMEM((NZ, ROWS, 2 * DIM), jnp.float32),
            pltpu.VMEM((2 * HEADS, LOCAL), jnp.float32),
            pltpu.VMEM((NG, 1, DIM), jnp.float32),
            pltpu.VMEM((NG, 1, DIM), jnp.float32),
            dma, dma,
            dma((NZ,)), dma((NZ,)), dma((NY,)), dma((NY,)),
            dma((NG,)), dma((NG,)), dma((NG,)), dma((NG,)),
            dma((NY,)), dma((NY,)), dma((NZ,)), dma((NZ,)),
        ],
        compiler_params=pltpu.CompilerParams(
            collective_id=0, has_side_effects=True, vmem_limit_bytes=40 * 2**20
        ),
        name="attend_and_migrate",
    )(page_table, context_len, mig_dest, query, key_value_scales[0], key_value_pages[0])
    attended = (
        att.reshape(RG, 2, STEPS, DIM).transpose(2, 0, 1, 3).reshape(STEPS, RG, 2 * DIM)
    )
    return attended, got_pages[None], got_scales[:, : 2 * HEADS].astype(jnp.bfloat16)[None]


def solution(mesh):
    return jax.shard_map(
        local,
        mesh=mesh,
        in_specs=(
            P(None, "group", "seq"),
            P("group", "seq", None, None),
            P("group", "seq", None),
            P("group", "seq", None),
            P("group"),
            P("group", "seq"),
        ),
        out_specs=(P(None, "group", "seq"), P("group", "seq", None, None), P("group", "seq", None)),
        check_vma=False,
    )
```

time: 537 us -> 136 us (0.25)
  the two profiles are of different devices: /device:TPU:12 before, /device:TPU:16 now
where the time goes in v1:
time: 136 us
  Pallas kernels  127 us (93%)
  local copies, waits for them, and re-layouts  7.49 us (6%)
    pallas_call x1, Pallas kernels, local(): pl.pallas_call(kernel, out_shape=(jax.ShapeDtypeStruct((ROWS, DIM), jnp.b...  127 us
    unnamed x11, local copies, waits for them, and re-layouts  5.58 us

profile of v1, /device:TPU:16, one launch (start us, length us, event | category | flops | bytes accessed | tf_op | source)
XLA Modules:
  0.0 135.6 jit_solution(10391206257045325602)
XLA Ops:
  0.6 0.7 reshape.18
  1.3 0.0 copy-start
  1.3 1.6 %copy-done = bf16[1,16,32,2048]{3,2,1,0:T(8,128)(2,1)S(1)} copy-done((bf16[1,16,32,2048]{3,2,1,0:T(8,128)(2,1)S(1)}, bf16[1,16,32,2048]{3,2,1,0:T(8,128)(2,1)}, u32[]{:S(2)}) %copy-start) | copy-done | bytes 2097176
  2.9 0.0 copy-start.1
  2.9 0.7 copy-done.1
  3.6 0.0 copy-start.2
  3.6 0.7 copy-done.2
  4.3 0.0 copy-start.3
  4.3 0.7 copy-done.3
  4.9 0.0 copy-start.4
  5.0 0.7 copy-done.4
  5.6 127.5 %attend_and_migrate.1 = (bf16[16,128]{1,0:T(8,128)(2,1)S(1)}, bf16[16,32,2048]{2,1,0:T(8,128)(2,1)S(1)}, f32[16,128]{1,0:T(8,128)S(1)}) custom-call(s32[1,1,16]{2,1,0:T(1,128)S(1)} %copy-done.3, s32[2]{0:T(128)S(1)} %copy-done.4, s32[2,8]{1,0:T(2,128)S(1)} %copy-done.2, bf16[16,128]{1,0:T(8,128)(2,1)S(1)} %bitcast.13, bf16[16,16]{1,0:T(8,128)(2,1)S(1)} %bitcast.14, ...), custom_call_target="tpu_custom_call" | custom-call | tf_op jit(solution)/shard_map/attend_and_migrate/pallas_call | solution.py:235
  133.1 0.6 reshape.21
  133.7 0.6 fusion
  134.3 1.3 copy.12
  (2 shorter events, 0.0 us)
Async XLA Ops:
  1.3 1.6 %copy-start = (bf16[1,16,32,2048]{3,2,1,0:T(8,128)(2,1)S(1)}, bf16[1,16,32,2048]{3,2,1,0:T(8,128)(2,1)}, u32[]{:S(2)}) copy-start(bf16[1,16,32,2048]{3,2,1,0:T(8,128)(2,1)} %param.7) | copy-start | bytes 6291460
  2.9 0.7 copy-start.1
  3.6 0.7 copy-start.2
  4.3 0.7 copy-start.3
  4.9 0.7 copy-start.4

commit v2 on v1

v2 whole, which is shorter than its diff:
```python
import functools

import jax
import jax.numpy as jnp
from jax import lax
from jax.experimental import pallas as pl
from jax.experimental.pallas import tpu as pltpu
from jax.sharding import PartitionSpec as P

NEGATIVE = -1e30
MESH = pl.DeviceIdType.MESH
NX, NH, NC, NZ, NY = 4, 2, 2, 8, 4
NG = NX * NH * NC
COLS = NX * NC
STEPS, RG, PPR, SLOTS, TOKENS = 4, 2, 8, 16, 32
HEADS, DIM = 8, 128
WIDTH = 2 * HEADS * DIM
LOCAL = SLOTS * TOKENS
ROWS = 16
STRIPE = WIDTH // COLS
PARTS, PART_ROWS, PART_COLS = 4, 16, 128
PAIRS = COLS * COLS
ROOM = (16, 25, 36, PAIRS)


def join(parts):
    context = parts[..., :DIM]
    highest = parts[..., DIM : DIM + 1]
    totals = parts[..., DIM + 1 : DIM + 2]
    top = jnp.max(highest, axis=0)
    factor = jnp.exp(highest - top[None])
    return jnp.sum(context * factor, axis=0), top, jnp.sum(totals * factor, axis=0)


def with_stats(top, total):
    lane = lax.broadcasted_iota(jnp.int32, top.shape[:-1] + (DIM,), top.ndim - 1)
    return jnp.where(lane == 0, top, total)


def group_of(column, half):
    return ((column // NC) * NH + half) * NC + column % NC


class Place:
    def __init__(self):
        self.g = lax.axis_index("group")
        self.s = lax.axis_index("seq")
        self.x, self.zh, self.c = self.g // (NH * NC), (self.g // NC) % NH, self.g % NC
        self.zl, self.y = self.s // NY, self.s % NY
        self.column = self.x * NC + self.c

    def along_z(self, d):
        return (self.g, lax.rem(self.zl + d, NZ) * NY + self.y)

    def along_y(self, d):
        return (self.g, self.zl * NY + lax.rem(self.y + d, NY))

    def column_at(self, d):
        return lax.rem(self.x + d // NC, NX) * NC + lax.rem(self.c + d % NC, NC)


def remote(src, dst, send_sem, recv_sem, device):
    return pltpu.make_async_remote_copy(
        src, dst, send_sem, recv_sem, device_id=device, device_id_type=MESH
    )


def greet(devices):
    barrier = pltpu.get_barrier_semaphore()
    for device in devices:
        pl.semaphore_signal(barrier, 1, device_id=device, device_id_type=MESH)
    pl.semaphore_wait(barrier, len(devices))


def first_kernel(
    table_in, ctx_in, mig_in, query_in, scales_in, pages_in,
    packed_out, half_out, flags_out, count_out, zpart_out, scales_out,
    table, ctx, mig, query, scales, pool, half, stripes, relay, packed,
    qall, part, yland, scale_rows, sc_send, sc_recv, fl_send, fl_recv, flags,
    cz, cy, count, following, index,
    in_sem, out_sem,
    zq_s, zq_r, yq_s, yq_r, st_s, st_r, sc_s, sc_r, fl_s, fl_r, yr_s, yr_r, cz_s, cz_r, cy_s, cy_r,
):
    here = Place()
    g, s, zh, zl, y, column = here.g, here.s, here.zh, here.zl, here.y, here.column
    loads = [
        pltpu.make_async_copy(a, b, in_sem.at[i])
        for i, (a, b) in enumerate(
            [(mig_in, mig), (table_in, table), (query_in, query), (pages_in, pool), (scales_in, scales), (ctx_in, ctx)]
        )
    ]
    for copy in loads:
        copy.start()

    group_peers = [
        (group_of(here.column_at(d % COLS), lax.rem(zh + d // COLS, NH)), s) for d in range(1, NG)
    ]
    greet(
        group_peers
        + [here.along_z(d) for d in range(1, NZ)]
        + [here.along_y(d) for d in range(1, NY)]
    )

    for copy in loads[:3]:
        copy.wait()
    lane = lax.broadcasted_iota(jnp.int32, (1, DIM), 1)
    row_flags = jnp.zeros((1, DIM), jnp.int32)
    for r in range(RG):
        for j in range(PPR):
            row_flags = jnp.where((lane == mig[r, j]) & (lane != g), 1, row_flags)
    fl_send[...] = row_flags
    fl_recv[g] = row_flags
    flag_copies = []
    for d, peer in enumerate(group_peers, 1):
        copy = remote(fl_send, fl_recv.at[g], fl_s.at[d], fl_r.at[d], peer)
        copy.start()
        flag_copies.append(copy)

    z_queries = []
    for d in range(1, NZ):
        copy = remote(query, qall.at[y, zl], zq_s.at[d], zq_r.at[d], here.along_z(d))
        copy.start()
        z_queries.append(copy)
    qall[y, zl] = query[...]

    def page_for(h):
        found, slot = jnp.int32(0), jnp.int32(0)
        for r in range(RG):
            for j in range(PPR):
                mine = mig[r, j] == h
                slot = jnp.where(mine, table[0, 0, r * PPR + j], slot)
                found = jnp.where(mine, 1, found)
        return jnp.where(h == g, 0, found), slot

    loads[3].wait()

    def cut_page(b, carry):
        found, slot = page_for(group_of(b, 1 - zh))
        value = pool[slot]
        value = jnp.where(found > 0, value, jnp.zeros_like(value))
        for i in range(COLS):
            stripes[i, b] = value[:, i * STRIPE : (i + 1) * STRIPE]
        return carry

    lax.fori_loop(0, COLS, cut_page, 0)
    stripe_copies = []
    for d in range(1, COLS):
        i = here.column_at(d)
        copy = remote(
            stripes.at[i], relay.at[pl.ds(column * COLS, COLS)], st_s.at[d], st_r.at[d],
            (group_of(i, zh), s),
        )
        copy.start()
        stripe_copies.append(copy)
    relay[pl.ds(column * COLS, COLS)] = stripes[column]

    def half_page(b, carry):
        found, slot = page_for(group_of(b, zh))
        value = pool[slot]
        half[b] = jnp.where(found > 0, value, jnp.zeros_like(value))
        return carry

    lax.fori_loop(0, COLS, half_page, 0)
    half_copy = pltpu.make_async_copy(half, half_out, out_sem.at[0])
    half_copy.start()

    loads[4].wait()
    slot_iota = lax.broadcasted_iota(jnp.int32, (NG, SLOTS), 1)
    dest_iota = lax.broadcasted_iota(jnp.int32, (NG, SLOTS), 0)
    chosen = jnp.zeros((NG, SLOTS), jnp.float32)
    token = lax.broadcasted_iota(jnp.int32, (8, LOCAL), 1)
    token_slot, token_in = token // TOKENS, token % TOKENS
    position = jnp.zeros((8, LOCAL), jnp.int32)
    owner = jnp.zeros((8, LOCAL), jnp.int32)
    for r in range(RG):
        for j in range(PPR):
            slot = table[0, 0, r * PPR + j]
            chosen = jnp.where(
                (dest_iota == mig[r, j]) & (slot_iota == slot) & (dest_iota != g), 1.0, chosen
            )
            mine = token_slot == slot
            position = jnp.where(mine, (j * NZ * NY + s) * TOKENS + token_in, position)
            owner = jnp.where(mine, r, owner)
    own_scales = scales[...]
    rows = jnp.dot(chosen.astype(jnp.bfloat16), own_scales, preferred_element_type=jnp.float32)
    rows = jnp.concatenate([rows, jnp.zeros((NG, DIM - 2 * HEADS), jnp.float32)], axis=1)
    for h in range(NG):
        sc_send[h] = rows[h : h + 1]
    sc_recv[g] = jnp.zeros((1, DIM), jnp.float32)
    scale_copies = []
    for d, peer in enumerate(group_peers, 1):
        copy = remote(sc_send.at[peer[0]], sc_recv.at[g], sc_s.at[d], sc_r.at[d], peer)
        copy.start()
        scale_copies.append(copy)

    for copy in flag_copies:
        copy.wait()
    flag_copy = pltpu.make_async_copy(fl_recv, flags, out_sem.at[1])
    flag_copy.start()
    source = lax.broadcasted_iota(jnp.int32, (NG, 1, DIM), 0)
    dest = lax.broadcasted_iota(jnp.int32, (NG, 1, DIM), 2)
    source_half, dest_half = (source // NC) % NH, (dest // NC) % NH
    sent = fl_recv[...].astype(jnp.float32)
    crossing = jnp.where(source_half != dest_half, sent, 0.0)
    per_half = [
        jnp.sum(jnp.sum(jnp.where(source_half == h, crossing, 0.0), axis=0), axis=1, keepdims=True)
        for h in range(NH)
    ]
    count[...] = jnp.broadcast_to(jnp.maximum(per_half[0], per_half[1]), (1, DIM))
    z_counts = []
    for d in range(1, NZ):
        copy = remote(count, cz.at[zl], cz_s.at[d], cz_r.at[d], here.along_z(d))
        copy.start()
        z_counts.append(copy)
    cz[zl] = count[...]

    for copy in z_queries:
        copy.wait()
    y_queries = []
    for d in range(1, NY):
        copy = remote(qall.at[y], qall.at[y], yq_s.at[d], yq_r.at[d], here.along_y(d))
        copy.start()
        y_queries.append(copy)

    loads[5].wait()
    spread = (
        lax.broadcasted_iota(jnp.int32, (SLOTS, LOCAL), 1) // TOKENS
        == lax.broadcasted_iota(jnp.int32, (SLOTS, LOCAL), 0)
    )
    scale_rows[...] = lax.dot_general(
        own_scales, jnp.where(spread, 1.0, 0.0).astype(jnp.bfloat16),
        (((0,), (0,)), ((), ())), preferred_element_type=jnp.float32,
    )
    row = lax.broadcasted_iota(jnp.int32, (NY * ROWS, LOCAL), 0)
    row_request, row_step = (row // 8) % RG, row % STEPS
    limit = jnp.where(row_request == 0, ctx[0], ctx[1]) - STEPS + 1 + row_step
    visible = (position[:1] < limit) & (owner[:1] == row_request)

    flag_copy.wait()
    following[PAIRS] = PAIRS - 1

    def look_back(i, carry):
        pair = PAIRS - 1 - i
        present = flags[group_of(pair // COLS, zh), 0, group_of(pair % COLS, 1 - zh)]
        following[pair] = jnp.where(present > 0, pair, following[pair + 1])
        return carry

    lax.fori_loop(0, PAIRS, look_back, 0)

    def list_pairs(i, cursor):
        pair = following[cursor]
        index[i] = pair
        return jnp.minimum(pair + 1, PAIRS)

    lax.fori_loop(0, PAIRS, list_pairs, jnp.int32(0))

    for copy in z_counts:
        copy.wait()
    count[...] = jnp.max(cz[...], axis=0)
    y_counts = []
    for d in range(1, NY):
        copy = remote(count, cy.at[y], cy_s.at[d], cy_r.at[d], here.along_y(d))
        copy.start()
        y_counts.append(copy)
    cy[y] = count[...]

    for copy in y_queries:
        copy.wait()
    for k in range(HEADS):
        query_rows = qall[:, k].reshape(NY * ROWS, DIM)
        keys = pool[:, :, k * DIM : (k + 1) * DIM].reshape(LOCAL, DIM)
        values = pool[:, :, (HEADS + k) * DIM : (HEADS + k + 1) * DIM].reshape(LOCAL, DIM)
        raw = lax.dot_general(
            query_rows, keys, (((1,), (1,)), ((), ())), preferred_element_type=jnp.float32
        )
        scores = raw * (scale_rows[k : k + 1, :] * DIM**-0.5)
        top = jnp.max(jnp.where(visible, scores, NEGATIVE), axis=1, keepdims=True)
        terms = jnp.where(visible, jnp.exp(scores - top), 0.0)
        total = jnp.sum(terms, axis=1, keepdims=True)
        weights = (terms * scale_rows[HEADS + k : HEADS + k + 1, :]).astype(jnp.bfloat16)
        context = jnp.dot(weights, values, preferred_element_type=jnp.float32)
        part[:, k, :, :DIM] = context.reshape(NY, ROWS, DIM)
        part[:, k, :, DIM:] = with_stats(top, total).reshape(NY, ROWS, DIM)

    y_parts = []
    for d in range(1, NY):
        to = lax.rem(y + d, NY)
        copy = remote(part.at[to], yland.at[y], yr_s.at[d], yr_r.at[d], here.along_y(d))
        copy.start()
        y_parts.append(copy)
    yland[y] = part[y]

    for copy in stripe_copies:
        copy.wait()

    def pack(i, carry):
        stripe = relay[index[i]]
        for p in range(PARTS):
            r0, c0 = (p // 2) * PART_ROWS, (p % 2) * PART_COLS
            packed[p, i] = stripe[r0 : r0 + PART_ROWS, c0 : c0 + PART_COLS]
        return carry

    lax.fori_loop(0, PAIRS, pack, 0)
    packed_copy = pltpu.make_async_copy(packed, packed_out, out_sem.at[2])
    packed_copy.start()
    flags_out[...] = fl_recv[...]

    for copy in y_parts:
        copy.wait()
    for k in range(HEADS):
        context, top, total = join(yland[:, k])
        zpart_out[k, :, :DIM] = context
        zpart_out[k, :, DIM:] = with_stats(top, total)

    for copy in scale_copies:
        copy.wait()
    for h in range(NG):
        scales_out[h : h + 1, :] = sc_recv[h]
    for copy in y_counts:
        copy.wait()
    count_out[...] = jnp.max(cy[...], axis=0)
    half_copy.wait()
    packed_copy.wait()


def second_kernel(
    room, packed, half, flags_in, zpart,
    att, out_pages,
    flags, rank, crossed_0, crossed_1, crossed_2, crossed_3, handed, zland, flag_sem, own_sem,
    cr_s, cr_r, ha_s, ha_r, hd_s, hd_r, zr_s, zr_r,
):
    crossed = (crossed_0, crossed_1, crossed_2, crossed_3)
    here = Place()
    g, s, zh, zl, column = here.g, here.s, here.zh, here.zl, here.column
    flag_copy = pltpu.make_async_copy(flags_in, flags, flag_sem)
    flag_copy.start()
    partner = (group_of(column, 1 - zh), s)
    peers = [here.column_at(d) for d in range(1, COLS)]
    greet(
        [partner]
        + [(group_of(i, zh), s) for i in peers]
        + [here.along_z(d) for d in range(1, NZ)]
    )

    crossings = []
    for p in range(PARTS):
        copy = remote(
            packed.at[p, pl.ds(0, room)], crossed[p], cr_s.at[p], cr_r.at[p], partner
        )
        copy.start()
        crossings.append(copy)

    z_parts = []
    for d in range(1, NZ):
        to = lax.rem(zl + d, NZ)
        copy = remote(zpart.at[to], zland.at[zl], zr_s.at[d], zr_r.at[d], here.along_z(d))
        copy.start()
        z_parts.append(copy)
    zland[zl] = zpart[zl]

    halves = []
    for d, i in enumerate(peers, 1):
        copy = remote(
            half.at[i], out_pages.at[here.x, zh, here.c], ha_s.at[d], ha_r.at[d], (group_of(i, zh), s)
        )
        copy.start()
        halves.append(copy)
    own_half = pltpu.make_async_copy(half.at[column], out_pages.at[here.x, zh, here.c], own_sem.at[PARTS])
    own_half.start()

    flag_copy.wait()

    def count_up(pair, before):
        present = flags[group_of(pair // COLS, 1 - zh), 0, group_of(pair % COLS, zh)]
        rank[pair] = jnp.where(present > 0, before, -1)
        return before + present

    lax.fori_loop(0, PAIRS, count_up, jnp.int32(0))

    handing, own_parts = [], []
    for p in range(PARTS):
        if p == PARTS // 2:
            for copy in z_parts:
                copy.wait()
            context, top, total = join(zland[...])
            att[...] = (context / total).astype(jnp.bfloat16)
        crossings[p].wait()

        def unpack(pair, carry):
            at = rank[pair]
            value = crossed[p][jnp.clip(at, 0, room - 1)]
            value = jnp.where(at >= 0, value, jnp.zeros_like(value))
            handed[p, pair % COLS, pair // COLS // NC, pair // COLS % NC] = value
            return carry

        lax.fori_loop(0, PAIRS, unpack, 0)
        r0, c0 = (p // 2) * PART_ROWS, (p % 2) * PART_COLS
        columns = pl.ds(pl.multiple_of(column * STRIPE + c0, PART_COLS), PART_COLS)
        target = out_pages.at[:, 1 - zh, :, pl.ds(r0, PART_ROWS), columns]
        for d, i in enumerate(peers, 1):
            copy = remote(handed.at[p, i], target, hd_s.at[p, d], hd_r.at[p, d], (group_of(i, zh), s))
            copy.start()
            handing.append(copy)
        copy = pltpu.make_async_copy(handed.at[p, column], target, own_sem.at[p])
        copy.start()
        own_parts.append(copy)

    for copy in halves + handing + [own_half] + own_parts:
        copy.wait()


dma = pltpu.SemaphoreType.DMA
vmem = pl.BlockSpec(memory_space=pltpu.VMEM)
hbm = pl.BlockSpec(memory_space=pl.ANY)


def second(room, identity):
    return pl.pallas_call(
        functools.partial(second_kernel, room),
        out_shape=(
            jax.ShapeDtypeStruct((ROWS, DIM), jnp.bfloat16),
            jax.ShapeDtypeStruct((NX, NH, NC, TOKENS, WIDTH), jnp.bfloat16),
        ),
        in_specs=[hbm, hbm, hbm, vmem],
        out_specs=(vmem, hbm),
        scratch_shapes=[
            pltpu.SMEM((NG, 1, DIM), jnp.int32),
            pltpu.SMEM((PAIRS,), jnp.int32),
            *[pltpu.VMEM((room, PART_ROWS, PART_COLS), jnp.bfloat16)] * PARTS,
            pltpu.VMEM((PARTS, COLS, NX, NC, PART_ROWS, PART_COLS), jnp.bfloat16),
            pltpu.VMEM((NZ, ROWS, 2 * DIM), jnp.float32),
            dma, dma((PARTS + 1,)),
            dma((PARTS,)), dma((PARTS,)), dma((COLS,)), dma((COLS,)),
            dma((PARTS, COLS)), dma((PARTS, COLS)), dma((NZ,)), dma((NZ,)),
        ],
        compiler_params=pltpu.CompilerParams(
            collective_id=identity, has_side_effects=True, vmem_limit_bytes=40 * 2**20
        ),
        name=f"cross_{room}",
    )


def local(queries, key_value_pages, key_value_scales, page_table, context_len, mig_dest):
    query = queries.reshape(STEPS, RG, 2, DIM).transpose(1, 2, 0, 3).reshape(ROWS, DIM)
    f32, bf16, i32 = jnp.float32, jnp.bfloat16, jnp.int32
    packed, half, flags, count, zpart, got_scales = pl.pallas_call(
        first_kernel,
        out_shape=(
            jax.ShapeDtypeStruct((PARTS, PAIRS, PART_ROWS, PART_COLS), bf16),
            jax.ShapeDtypeStruct((COLS, TOKENS, WIDTH), bf16),
            jax.ShapeDtypeStruct((NG, 1, DIM), i32),
            jax.ShapeDtypeStruct((1, DIM), f32),
            jax.ShapeDtypeStruct((NZ, ROWS, 2 * DIM), f32),
            jax.ShapeDtypeStruct((NG, DIM), f32),
        ),
        in_specs=[hbm] * 6,
        out_specs=(hbm, hbm, vmem, vmem, vmem, vmem),
        scratch_shapes=[
            pltpu.SMEM(page_table.shape, i32),
            pltpu.SMEM(context_len.shape, i32),
            pltpu.SMEM(mig_dest.shape, i32),
            pltpu.VMEM((ROWS, DIM), bf16),
            pltpu.VMEM((SLOTS, 2 * HEADS), bf16),
            pltpu.VMEM((SLOTS, TOKENS, WIDTH), bf16),
            pltpu.VMEM((COLS, TOKENS, WIDTH), bf16),
            pltpu.VMEM((COLS, COLS, TOKENS, STRIPE), bf16),
            pltpu.VMEM((PAIRS, TOKENS, STRIPE), bf16),
            pltpu.VMEM((PARTS, PAIRS, PART_ROWS, PART_COLS), bf16),
            pltpu.VMEM((NY, NZ, ROWS, DIM), bf16),
            pltpu.VMEM((NY, NZ, ROWS, 2 * DIM), f32),
            pltpu.VMEM((NY, NZ, ROWS, 2 * DIM), f32),
            pltpu.VMEM((2 * HEADS, LOCAL), f32),
            pltpu.VMEM((NG, 1, DIM), f32),
            pltpu.VMEM((NG, 1, DIM), f32),
            pltpu.VMEM((1, DIM), i32),
            pltpu.VMEM((NG, 1, DIM), i32),
            pltpu.SMEM((NG, 1, DIM), i32),
            pltpu.VMEM((NZ, 1, DIM), f32),
            pltpu.VMEM((NY, 1, DIM), f32),
            pltpu.VMEM((1, DIM), f32),
            pltpu.SMEM((PAIRS + 1,), i32),
            pltpu.SMEM((PAIRS,), i32),
            dma((6,)), dma((3,)),
            dma((NZ,)), dma((NZ,)), dma((NY,)), dma((NY,)), dma((COLS,)), dma((COLS,)),
            dma((NG,)), dma((NG,)), dma((NG,)), dma((NG,)), dma((NY,)), dma((NY,)),
            dma((NZ,)), dma((NZ,)), dma((NY,)), dma((NY,)),
        ],
        compiler_params=pltpu.CompilerParams(
            collective_id=0, has_side_effects=True, vmem_limit_bytes=40 * 2**20
        ),
        name="attend_and_pack",
    )(page_table, context_len, mig_dest, query, key_value_scales[0], key_value_pages[0])
    most = count[0, 0]
    choice = sum((most > room).astype(i32) for room in ROOM[:-1])
    att, got_pages = lax.switch(
        choice, [second(room, 1 + i) for i, room in enumerate(ROOM)], packed, half, flags, zpart
    )
    attended = (
        att.reshape(RG, 2, STEPS, DIM).transpose(2, 0, 1, 3).reshape(STEPS, RG, 2 * DIM)
    )
    return (
        attended,
        got_pages.reshape(1, NG, TOKENS, WIDTH),
        got_scales[:, : 2 * HEADS].astype(bf16)[None],
    )


def solution(mesh):
    return jax.shard_map(
        local,
        mesh=mesh,
        in_specs=(
            P(None, "group", "seq"),
            P("group", "seq", None, None),
            P("group", "seq", None),
            P("group", "seq", None),
            P("group"),
            P("group", "seq"),
        ),
        out_specs=(P(None, "group", "seq"), P("group", "seq", None, None), P("group", "seq", None)),
        check_vma=False,
    )
```

time: 136 us -> 98.5 us (0.72)
  the two profiles are of different devices: /device:TPU:16 before, /device:TPU:1 now
where the time goes in v2:
time: 98.5 us; the launch traced here: 98.2 us
  Pallas kernels  88 us (89%)
  local copies, waits for them, and re-layouts  9.33 us (9%)
    pallas_call x1, Pallas kernels, local(): lax.switch(choice, [second(room, 1 + i) for i, room in enumerate(ROOM)],...  46.9 us
    pallas_call x1, Pallas kernels, local(): pl.pallas_call(first_kernel, out_shape=(jax.ShapeDtypeStruct((PARTS, PAIR...  41.1 us
    unnamed x11, local copies, waits for them, and re-layouts  7.42 us

profile of v2, /device:TPU:1, one launch (start us, length us, event | category | flops | bytes accessed | tf_op | source)
XLA Modules:
  0.0 98.2 jit_solution(11361818027804698396)
XLA Ops:
  0.6 0.7 reshape.42
  1.3 0.0 copy-start
  1.3 1.6 %copy-done = bf16[1,16,32,2048]{3,2,1,0:T(8,128)(2,1)S(1)} copy-done((bf16[1,16,32,2048]{3,2,1,0:T(8,128)(2,1)S(1)}, bf16[1,16,32,2048]{3,2,1,0:T(8,128)(2,1)}, u32[]{:S(2)}) %copy-start) | copy-done | bytes 2097176
  2.9 0.0 copy-start.1
  2.9 0.7 copy-done.1
  3.6 0.0 copy-start.2
  3.6 0.7 copy-done.2
  4.3 0.0 copy-start.3
  4.3 0.7 copy-done.3
  4.9 0.0 copy-start.4
  5.0 0.7 copy-done.4
  5.6 41.1 %attend_and_pack.1 = (bf16[4,64,16,128]{3,2,1,0:T(8,128)(2,1)S(1)}, bf16[8,32,2048]{2,1,0:T(8,128)(2,1)S(1)}, s32[16,1,128]{2,1,0:T(1,128)S(1)}, f32[1,128]{1,0:...) custom-call(s32[1,1,16]{2,1,0:T(1,128)S(1)} %copy-done.3, s32[2]{0:T(128)S(1)} %copy-done.4, ...), custom_call_target="tpu_custom_call" | custom-call | tf_op jit(solution)/shard_map/attend_and_pack/pallas_call | solution.py:446
  46.9 46.9 %conditional.1 = (bf16[16,128]{1,0:T(8,128)(2,1)S(1)}, bf16[1,16,32,2048]{3,2,1,0:T(8,128)(2,1)}) conditional(s32[]{:T(128)} %bitcast.8, (bf16[4,64,16,128]{3,2,1,0:T(8,128)(2,1)S(1)}, bf16[8,32,2048]{2,1,0:T(8,128)(2,1)S(1)}, s32[16,1,128]{2,1,0:T(1,128)S(1)}, f32[8,16,256]{2,1,0:T(8,128)S(1)}) %tuple.28, ...), branch_computations={%region_0.0_spmd, %region_1.0_spmd, %region_2.0_spmd, %region_3.0_... | conditional | bytes 16 | solution.py:495
  46.9 46.9 %cross_16.1 = (bf16[16,128]{1,0:T(8,128)(2,1)S(1)}, bf16[4,2,2,32,2048]{4,3,2,1,0:T(8,128)(2,1)}) custom-call(bf16[4,64,16,128]{3,2,1,0:T(8,128)(2,1)S(1)} %get-tuple-element.41.packed, bf16[8,32,2048]{2,1,0:T(8,128)(2,1)S(1)} %get-tuple-element.42.half, s32[16,1,128]{2,1,0:T(1,128)S(1)} %get-tuple-element.43.flags_in, f32[8,16,256]{2,1,0:T(8,128)S(1)} %get-tuple-element.44.zpart), custom_call_target="tpu_custom_call" | custom-call | tf_op jit(solution)/shard_map/cond/branch_0_fun/cross_16/pallas_call | solution.py:495
  93.8 0.6 reshape.45
  94.4 0.6 fusion
  95.0 3.2 %copy.22 = bf16[1,16,32,2048]{3,2,1,0:T(8,128)(2,1)} copy(bf16[1,16,32,2048]{3,2,1,0:T(8,128)(2,1)} %get-tuple-element.96) | data formatting | bytes 4194304
  (2 shorter events, 0.0 us)
Async XLA Ops:
  1.3 1.6 %copy-start = (bf16[1,16,32,2048]{3,2,1,0:T(8,128)(2,1)S(1)}, bf16[1,16,32,2048]{3,2,1,0:T(8,128)(2,1)}, u32[]{:S(2)}) copy-start(bf16[1,16,32,2048]{3,2,1,0:T(8,128)(2,1)} %param.11) | copy-start | bytes 6291460
  2.9 0.7 copy-start.1
  3.6 0.7 copy-start.2
  4.3 0.7 copy-start.3
  4.9 0.7 copy-start.4

commit v3 on v1

v3 whole, which is shorter than its diff:
```python
import functools

import jax
import jax.numpy as jnp
from jax import lax
from jax.experimental import pallas as pl
from jax.experimental.pallas import tpu as pltpu
from jax.sharding import PartitionSpec as P

NEGATIVE = -1e30
MESH = pl.DeviceIdType.MESH
NX, NH, NC, NZ, NY = 4, 2, 2, 8, 4
NG = NX * NH * NC
COLS = NX * NC
STEPS, RG, PPR, SLOTS, TOKENS = 4, 2, 8, 16, 32
HEADS, DIM = 8, 128
WIDTH = 2 * HEADS * DIM
LOCAL = SLOTS * TOKENS
ROWS = 16
STRIPE = WIDTH // COLS
PARTS, PART_ROWS, PART_COLS = 4, 16, 128
PAIRS = COLS * COLS
FIRST = 16
ROOM = (25, 36, PAIRS)


def part_offsets(p):
    return (p // 2) * PART_ROWS, (p % 2) * PART_COLS


def split(value):
    high = value.astype(jnp.bfloat16).astype(jnp.float32)
    middle = (value - high).astype(jnp.bfloat16).astype(jnp.float32)
    return high, middle, value - high - middle


def with_lanes(base, first, spacing, value):
    lane = lax.broadcasted_iota(jnp.int32, base.shape, 1)
    for i, term in enumerate(split(value)):
        base = jnp.where(lane == first + i * spacing, term, base)
    return base


def join(contexts, levels):
    top = jnp.max(levels, axis=0)
    factor = jnp.exp(levels - top[None])
    total = jnp.sum(factor, axis=0)
    context = jnp.sum(contexts.astype(jnp.float32) * factor, axis=0) / total
    return context, jnp.maximum(top + jnp.log(total), NEGATIVE)


def group_of(column, half):
    return ((column // NC) * NH + half) * NC + column % NC


class Place:
    def __init__(self):
        self.g = lax.axis_index("group")
        self.s = lax.axis_index("seq")
        self.x, self.zh, self.c = self.g // (NH * NC), (self.g // NC) % NH, self.g % NC
        self.zl, self.y = self.s // NY, self.s % NY
        self.column = self.x * NC + self.c

    def along_z(self, d):
        return (self.g, lax.rem(self.zl + d, NZ) * NY + self.y)

    def along_y(self, d):
        return (self.g, self.zl * NY + lax.rem(self.y + d, NY))

    def column_at(self, d):
        return lax.rem(self.x + d // NC, NX) * NC + lax.rem(self.c + d % NC, NC)


def remote(src, dst, send_sem, recv_sem, device):
    copy = pltpu.make_async_remote_copy(
        src, dst, send_sem, recv_sem, device_id=device, device_id_type=MESH
    )
    copy.start()
    return copy


def inside(src, dst, sem):
    copy = pltpu.make_async_copy(src, dst, sem)
    copy.start()
    return copy


def wait(copies):
    for copy in copies:
        copy.wait()


def greet(devices):
    barrier = pltpu.get_barrier_semaphore()
    for device in devices:
        pl.semaphore_signal(barrier, 1, device_id=device, device_id_type=MESH)
    pl.semaphore_wait(barrier, len(devices))


def rank_pairs(flags, source_half, dest_half, rank):
    def count_up(pair, before):
        present = flags[pair // COLS, 0, group_of(pair % COLS, dest_half)]
        rank[pair] = jnp.where(present > 0, before, -1)
        return before + present

    lax.fori_loop(0, PAIRS, count_up, jnp.int32(0))


def hand_over(here, p, handed, out_pages, send_sems, recv_sems, own_sem):
    r0, c0 = part_offsets(p)
    columns = pl.ds(pl.multiple_of(here.column * STRIPE + c0, PART_COLS), PART_COLS)
    target = out_pages.at[:, 1 - here.zh, :, pl.ds(r0, PART_ROWS), columns]
    copies = []
    for d in range(1, COLS):
        i = here.column_at(d)
        copies.append(
            remote(
                handed.at[p, i], target, send_sems.at[p, d], recv_sems.at[p, d],
                (group_of(i, here.zh), here.s),
            )
        )
    copies.append(inside(handed.at[p, here.column], target, own_sem.at[p]))
    return copies


def first_kernel(
    table_in, ctx_in, mig_in, query_in, scales_in, pages_in,
    att_out, out_pages, scales_out, packed_out, crossed_out, same_out, other_out, count_out,
    table, ctx, mig, query, scales, pool, half, stripes, packed, handed,
    relay_0, relay_1, relay_2, relay_3, crossed_0, crossed_1, crossed_2, crossed_3,
    qmine, qall, ypart, yland, zpart, zland, scale_rows, sc_send, sc_recv, sc_all,
    fl_send, fl_same, fl_other, same, other, cz, cy, count,
    slots, found, following, index, rank,
    in_sem, out_sem, own_sem,
    zq_s, zq_r, yq_s, yq_r, st_s, st_r, cr_s, cr_r, ha_s, ha_r, hd_s, hd_r,
    sc_s, sc_r, fl_s, fl_r, yr_s, yr_r, zr_s, zr_r, cz_s, cz_r, cy_s, cy_r,
):
    relays = (relay_0, relay_1, relay_2, relay_3)
    crossed = (crossed_0, crossed_1, crossed_2, crossed_3)
    here = Place()
    g, s, zh, zl, y, column = here.g, here.s, here.zh, here.zl, here.y, here.column
    get_mig, get_table, get_query, get_pool, get_scales, get_ctx = [
        inside(a, b, in_sem.at[i])
        for i, (a, b) in enumerate(
            [(mig_in, mig), (table_in, table), (query_in, query), (pages_in, pool), (scales_in, scales), (ctx_in, ctx)]
        )
    ]
    same_peers = [(group_of(here.column_at(d), zh), s) for d in range(1, COLS)]
    other_peers = [(group_of(here.column_at(d), 1 - zh), s) for d in range(COLS)]
    z_peers = [here.along_z(d) for d in range(1, NZ)]
    y_peers = [here.along_y(d) for d in range(1, NY)]
    greet(same_peers + other_peers + z_peers + y_peers)

    get_mig.wait()
    lane = lax.broadcasted_iota(jnp.int32, (1, DIM), 1)
    row_flags = jnp.zeros((1, DIM), jnp.int32)
    for r in range(RG):
        for j in range(PPR):
            row_flags = jnp.where((lane == mig[r, j]) & (lane != g), 1, row_flags)
    fl_send[...] = row_flags
    fl_same[column] = row_flags
    same_flags = [
        remote(fl_send, fl_same.at[column], fl_s.at[d], fl_r.at[d], peer)
        for d, peer in enumerate(same_peers, 1)
    ]
    other_flags = [
        remote(fl_send, fl_other.at[column], fl_s.at[COLS + d], fl_r.at[COLS + d], peer)
        for d, peer in enumerate(other_peers)
    ]

    get_query.wait()
    mine = query[...].astype(jnp.float32)
    mine = jnp.concatenate(
        [
            mine[t, r : r + 1, hh * DIM : (hh + 1) * DIM]
            for r in range(RG) for hh in range(2) for t in range(STEPS)
        ],
        axis=0,
    ).astype(jnp.bfloat16)
    qmine[...] = mine
    qall[y, zl] = mine
    z_queries = [
        remote(qmine, qall.at[y, zl], zq_s.at[d], zq_r.at[d], peer) for d, peer in enumerate(z_peers, 1)
    ]

    get_table.wait()

    def find_pages(i, carry):
        h = group_of(i % COLS, jnp.where(i < COLS, 1 - zh, zh))
        here_too, slot = jnp.int32(0), jnp.int32(0)
        for r in range(RG):
            for j in range(PPR):
                hit = mig[r, j] == h
                slot = jnp.where(hit, table[0, 0, r * PPR + j], slot)
                here_too = jnp.where(hit, 1, here_too)
        slots[i] = slot
        found[i] = jnp.where(h == g, 0, here_too)
        return carry

    lax.fori_loop(0, 2 * COLS, find_pages, 0)
    get_pool.wait()
    stripe_copies = []
    for p in range(PARTS):
        r0, c0 = part_offsets(p)

        def cut_page(b, carry):
            value = pool[slots[b], r0 : r0 + PART_ROWS]
            value = jnp.where(found[b] > 0, value, jnp.zeros_like(value))
            for i in range(COLS):
                start = i * STRIPE + c0
                stripes[p, i, b] = value[:, start : start + PART_COLS]
            return carry

        lax.fori_loop(0, COLS, cut_page, 0)
        place = relays[p].at[pl.ds(column * COLS, COLS)]
        stripe_copies.append(
            [
                remote(stripes.at[p, here.column_at(d)], place, st_s.at[p, d], st_r.at[p, d], peer)
                for d, peer in enumerate(same_peers, 1)
            ]
        )
        relays[p][pl.ds(column * COLS, COLS)] = stripes[p, column]

    wait(same_flags)
    inside(fl_same, same, out_sem.at[0]).wait()
    following[PAIRS] = PAIRS - 1

    def look_back(i, carry):
        pair = PAIRS - 1 - i
        present = same[pair // COLS, 0, group_of(pair % COLS, 1 - zh)]
        following[pair] = jnp.where(present > 0, pair, following[pair + 1])
        return carry

    lax.fori_loop(0, PAIRS, look_back, 0)

    def list_pairs(i, cursor):
        pair = following[cursor]
        index[i] = pair
        return jnp.minimum(pair + 1, PAIRS)

    lax.fori_loop(0, PAIRS, list_pairs, jnp.int32(0))

    def pack(p, start, stop):
        def step(i, carry):
            packed[p, i] = relays[p][index[i]]
            return carry

        lax.fori_loop(start, stop, step, 0)

    crossings, y_queries, z_counts = [], [], []
    for p in range(PARTS):
        wait(stripe_copies[p])
        pack(p, 0, FIRST)
        crossings.append(
            remote(packed.at[p, pl.ds(0, FIRST)], crossed[p], cr_s.at[p], cr_r.at[p], other_peers[0])
        )
        if p == 0:
            wait(z_queries)
            y_queries = [
                remote(qall.at[y], qall.at[y], yq_s.at[d], yq_r.at[d], peer)
                for d, peer in enumerate(y_peers, 1)
            ]
        if p == 1:
            wait(other_flags)
            source = lax.broadcasted_iota(jnp.int32, (COLS, 1, DIM), 2)
            dest_half = (source // NC) % NH
            per_half = [
                jnp.sum(
                    jnp.sum(jnp.where(dest_half != h, rows[...].astype(jnp.float32), 0.0), axis=0),
                    axis=1, keepdims=True,
                )
                for rows, h in ((fl_same, zh), (fl_other, 1 - zh))
            ]
            count[...] = jnp.broadcast_to(jnp.maximum(per_half[0], per_half[1]), (1, DIM))
            cz[zl] = count[...]
            z_counts = [
                remote(count, cz.at[zl], cz_s.at[d], cz_r.at[d], peer) for d, peer in enumerate(z_peers, 1)
            ]
    other_copy = inside(fl_other, other, out_sem.at[1])

    def half_page(b, carry):
        value = pool[slots[COLS + b]]
        half[b] = jnp.where(found[COLS + b] > 0, value, jnp.zeros_like(value))
        return carry

    lax.fori_loop(0, COLS, half_page, 0)
    own_place = out_pages.at[here.x, zh, here.c]
    halves = [
        remote(half.at[here.column_at(d)], own_place, ha_s.at[d], ha_r.at[d], peer)
        for d, peer in enumerate(same_peers, 1)
    ]
    halves.append(inside(half.at[column], own_place, out_sem.at[2]))

    get_scales.wait()
    get_ctx.wait()
    slot_iota = lax.broadcasted_iota(jnp.int32, (NG, SLOTS), 1)
    dest_iota = lax.broadcasted_iota(jnp.int32, (NG, SLOTS), 0)
    chosen = jnp.zeros((NG, SLOTS), jnp.float32)
    token = lax.broadcasted_iota(jnp.int32, (8, LOCAL), 1)
    token_slot, token_in = token // TOKENS, token % TOKENS
    position = jnp.zeros((8, LOCAL), jnp.int32)
    owner = jnp.zeros((8, LOCAL), jnp.int32)
    for r in range(RG):
        for j in range(PPR):
            slot = table[0, 0, r * PPR + j]
            chosen = jnp.where(
                (dest_iota == mig[r, j]) & (slot_iota == slot) & (dest_iota != g), 1.0, chosen
            )
            hit = token_slot == slot
            position = jnp.where(hit, (j * NZ * NY + s) * TOKENS + token_in, position)
            owner = jnp.where(hit, r, owner)
    own_scales = scales[...]
    rows = jnp.dot(chosen.astype(jnp.bfloat16), own_scales, preferred_element_type=jnp.float32)
    rows = jnp.concatenate([rows, jnp.zeros((NG, DIM - 2 * HEADS), jnp.float32)], axis=1)
    for h in range(NG):
        sc_send[h] = rows[h : h + 1]
    sc_recv[g] = jnp.zeros((1, DIM), jnp.float32)
    scale_copies = [
        remote(sc_send.at[peer[0]], sc_recv.at[g], sc_s.at[d], sc_r.at[d], peer)
        for d, peer in enumerate(other_peers + same_peers)
    ]
    spread = (
        lax.broadcasted_iota(jnp.int32, (SLOTS, LOCAL), 1) // TOKENS
        == lax.broadcasted_iota(jnp.int32, (SLOTS, LOCAL), 0)
    )
    scale_rows[...] = lax.dot_general(
        own_scales, jnp.where(spread, 1.0, 0.0).astype(jnp.bfloat16),
        (((0,), (0,)), ((), ())), preferred_element_type=jnp.float32,
    )
    row = lax.broadcasted_iota(jnp.int32, (NY * ROWS, LOCAL), 0)
    row_request, row_step = (row // 8) % RG, row % STEPS
    limit = jnp.where(row_request == 0, ctx[0], ctx[1]) - STEPS + 1 + row_step
    visible = (position[:1] < limit) & (owner[:1] == row_request)

    wait(y_queries)
    levels = jnp.zeros((NY * ROWS, DIM), jnp.float32)
    for k in range(HEADS):
        query_rows = qall[:, k].reshape(NY * ROWS, DIM)
        keys = pool[:, :, k * DIM : (k + 1) * DIM].reshape(LOCAL, DIM)
        values = pool[:, :, (HEADS + k) * DIM : (HEADS + k + 1) * DIM].reshape(LOCAL, DIM)
        raw = lax.dot_general(
            query_rows, keys, (((1,), (1,)), ((), ())), preferred_element_type=jnp.float32
        )
        scores = raw * (scale_rows[k : k + 1, :] * DIM**-0.5)
        top = jnp.max(jnp.where(visible, scores, NEGATIVE), axis=1, keepdims=True)
        terms = jnp.where(visible, jnp.exp(scores - top), 0.0)
        total = jnp.sum(terms, axis=1, keepdims=True)
        weights = (terms * scale_rows[HEADS + k : HEADS + k + 1, :]).astype(jnp.bfloat16)
        context = jnp.dot(weights, values, preferred_element_type=jnp.float32)
        some = total > 0.0
        total = jnp.where(some, total, 1.0)
        ypart[:, k] = (context / total).astype(jnp.bfloat16).reshape(NY, ROWS, DIM)
        levels = with_lanes(levels, k, HEADS, jnp.where(some, top + jnp.log(total), NEGATIVE))
    ypart[:, HEADS] = levels.astype(jnp.bfloat16).reshape(NY, ROWS, DIM)

    y_parts = [
        remote(ypart.at[lax.rem(y + d, NY)], yland.at[y], yr_s.at[d], yr_r.at[d], peer)
        for d, peer in enumerate(y_peers, 1)
    ]
    yland[y] = ypart[y]

    wait(z_counts)
    count[...] = jnp.max(cz[...], axis=0)
    cy[y] = count[...]
    y_counts = [
        remote(count, cy.at[y], cy_s.at[d], cy_r.at[d], peer) for d, peer in enumerate(y_peers, 1)
    ]

    for p in range(PARTS):
        pack(p, FIRST, PAIRS)
    outs = [inside(packed, packed_out, out_sem.at[3])]

    wait(y_parts)
    terms = yland[:, HEADS].astype(jnp.float32)
    for k in range(HEADS):
        level = sum(terms[:, :, k + i * HEADS : k + i * HEADS + 1] for i in range(3))
        context, level = join(yland[:, k], level)
        zpart[k, 0] = context.astype(jnp.bfloat16)
        zpart[k, 1] = with_lanes(jnp.zeros((ROWS, DIM), jnp.float32), 0, 1, level).astype(jnp.bfloat16)
    z_parts = [
        remote(zpart.at[lax.rem(zl + d, NZ)], zland.at[zl], zr_s.at[d], zr_r.at[d], peer)
        for d, peer in enumerate(z_peers, 1)
    ]
    zland[zl] = zpart[zl]

    other_copy.wait()
    rank_pairs(other, 1 - zh, zh, rank)
    handing = []
    for p in range(PARTS):
        crossings[p].wait()

        def unpack(pair, carry):
            at = rank[pair]
            value = crossed[p][jnp.clip(at, 0, FIRST - 1)]
            value = jnp.where((at >= 0) & (at < FIRST), value, jnp.zeros_like(value))
            handed[p, pair % COLS, pair // COLS // NC, pair // COLS % NC] = value
            return carry

        lax.fori_loop(0, PAIRS, unpack, 0)
        handing += hand_over(here, p, handed, out_pages, hd_s, hd_r, own_sem)
        outs.append(inside(crossed[p], crossed_out.at[p], out_sem.at[4 + p]))

    wait(z_parts)
    terms = zland[:, 1].astype(jnp.float32)
    context, _ = join(zland[:, 0], sum(terms[:, :, i : i + 1] for i in range(3)))
    for t in range(STEPS):
        att_out[t] = jnp.concatenate(
            [
                jnp.concatenate(
                    [
                        context[r * 8 + hh * STEPS + t : r * 8 + hh * STEPS + t + 1]
                        for hh in range(2)
                    ],
                    axis=1,
                )
                for r in range(RG)
            ],
            axis=0,
        ).astype(jnp.bfloat16)

    wait(scale_copies)
    for h in range(NG):
        sc_all[h : h + 1, :] = sc_recv[h]
    scales_out[...] = sc_all[:, : 2 * HEADS].astype(jnp.bfloat16)
    same_out[...] = fl_same[...]
    other_out[...] = fl_other[...]
    wait(y_counts)
    count_out[...] = jnp.max(cy[...], axis=0)
    wait(halves)
    wait(outs)
    wait(handing)


def second_kernel(
    room, packed, first_in, other_in, pages_before,
    out_pages,
    other, rank, first, rest_0, rest_1, rest_2, rest_3, handed, in_sem, own_sem,
    cr_s, cr_r, hd_s, hd_r,
):
    rest = (rest_0, rest_1, rest_2, rest_3)
    here = Place()
    get_other = inside(other_in, other, in_sem.at[0])
    get_first = inside(first_in, first, in_sem.at[1])
    partner = (group_of(here.column, 1 - here.zh), here.s)
    greet([partner] + [(group_of(here.column_at(d), here.zh), here.s) for d in range(1, COLS)])
    crossings = [
        remote(packed.at[p, pl.ds(FIRST, room - FIRST)], rest[p], cr_s.at[p], cr_r.at[p], partner)
        for p in range(PARTS)
    ]
    get_other.wait()
    rank_pairs(other, 1 - here.zh, here.zh, rank)
    get_first.wait()
    handing = []
    for p in range(PARTS):
        crossings[p].wait()

        def unpack(pair, carry):
            at = rank[pair]
            early = first[p, jnp.clip(at, 0, FIRST - 1)]
            late = rest[p][jnp.clip(at - FIRST, 0, room - FIRST - 1)]
            value = jnp.where(at < FIRST, early, late)
            value = jnp.where(at >= 0, value, jnp.zeros_like(value))
            handed[p, pair % COLS, pair // COLS // NC, pair // COLS % NC] = value
            return carry

        lax.fori_loop(0, PAIRS, unpack, 0)
        handing += hand_over(here, p, handed, out_pages, hd_s, hd_r, own_sem)
    wait(handing)


dma = pltpu.SemaphoreType.DMA
VMEM_BYTES = 63 * 2**20
f32, bf16, i32 = jnp.float32, jnp.bfloat16, jnp.int32
vmem = pl.BlockSpec(memory_space=pltpu.VMEM)
hbm = pl.BlockSpec(memory_space=pltpu.HBM)
PART = (PART_ROWS, PART_COLS)
PAGES = (NX, NH, NC, TOKENS, WIDTH)
HANDED = (PARTS, COLS, NX, NC) + PART


def second(room, identity):
    return pl.pallas_call(
        functools.partial(second_kernel, room),
        out_shape=jax.ShapeDtypeStruct(PAGES, bf16),
        in_specs=[hbm] * 4,
        out_specs=hbm,
        input_output_aliases={3: 0},
        scratch_shapes=[
            pltpu.SMEM((COLS, 1, DIM), i32),
            pltpu.SMEM((PAIRS,), i32),
            pltpu.VMEM((PARTS, FIRST) + PART, bf16),
            *[pltpu.VMEM((room - FIRST,) + PART, bf16)] * PARTS,
            pltpu.VMEM(HANDED, bf16),
            dma((2,)), dma((PARTS,)),
            dma((PARTS,)), dma((PARTS,)), dma((PARTS, COLS)), dma((PARTS, COLS)),
        ],
        compiler_params=pltpu.CompilerParams(
            collective_id=identity, has_side_effects=True, vmem_limit_bytes=VMEM_BYTES
        ),
        name=f"cross_{room}",
    )


def local(queries, key_value_pages, key_value_scales, page_table, context_len, mig_dest):
    att, got_pages, got_scales, packed, crossed, same, other, count = pl.pallas_call(
        first_kernel,
        out_shape=(
            jax.ShapeDtypeStruct(queries.shape, bf16),
            jax.ShapeDtypeStruct(PAGES, bf16),
            jax.ShapeDtypeStruct((NG, 2 * HEADS), bf16),
            jax.ShapeDtypeStruct((PARTS, PAIRS) + PART, bf16),
            jax.ShapeDtypeStruct((PARTS, FIRST) + PART, bf16),
            jax.ShapeDtypeStruct((COLS, 1, DIM), i32),
            jax.ShapeDtypeStruct((COLS, 1, DIM), i32),
            jax.ShapeDtypeStruct((1, DIM), f32),
        ),
        in_specs=[hbm] * 6,
        out_specs=(vmem, hbm, vmem, hbm, hbm, vmem, vmem, vmem),
        scratch_shapes=[
            pltpu.SMEM(page_table.shape, i32),
            pltpu.SMEM(context_len.shape, i32),
            pltpu.SMEM(mig_dest.shape, i32),
            pltpu.VMEM(queries.shape, bf16),
            pltpu.VMEM((SLOTS, 2 * HEADS), bf16),
            pltpu.VMEM((SLOTS, TOKENS, WIDTH), bf16),
            pltpu.VMEM((COLS, TOKENS, WIDTH), bf16),
            pltpu.VMEM((PARTS, COLS, COLS) + PART, bf16),
            pltpu.VMEM((PARTS, PAIRS) + PART, bf16),
            pltpu.VMEM(HANDED, bf16),
            *[pltpu.VMEM((PAIRS,) + PART, bf16)] * PARTS,
            *[pltpu.VMEM((FIRST,) + PART, bf16)] * PARTS,
            pltpu.VMEM((ROWS, DIM), bf16),
            pltpu.VMEM((NY, NZ, ROWS, DIM), bf16),
            pltpu.VMEM((NY, HEADS + 1, ROWS, DIM), bf16),
            pltpu.VMEM((NY, HEADS + 1, ROWS, DIM), bf16),
            pltpu.VMEM((NZ, 2, ROWS, DIM), bf16),
            pltpu.VMEM((NZ, 2, ROWS, DIM), bf16),
            pltpu.VMEM((2 * HEADS, LOCAL), f32),
            pltpu.VMEM((NG, 1, DIM), f32),
            pltpu.VMEM((NG, 1, DIM), f32),
            pltpu.VMEM((NG, DIM), f32),
            pltpu.VMEM((1, DIM), i32),
            pltpu.VMEM((COLS, 1, DIM), i32),
            pltpu.VMEM((COLS, 1, DIM), i32),
            pltpu.SMEM((COLS, 1, DIM), i32),
            pltpu.SMEM((COLS, 1, DIM), i32),
            pltpu.VMEM((NZ, 1, DIM), f32),
            pltpu.VMEM((NY, 1, DIM), f32),
            pltpu.VMEM((1, DIM), f32),
            pltpu.SMEM((2 * COLS,), i32),
            pltpu.SMEM((2 * COLS,), i32),
            pltpu.SMEM((PAIRS + 1,), i32),
            pltpu.SMEM((PAIRS,), i32),
            pltpu.SMEM((PAIRS,), i32),
            dma((6,)), dma((4 + PARTS,)), dma((PARTS,)),
            dma((NZ,)), dma((NZ,)), dma((NY,)), dma((NY,)),
            dma((PARTS, COLS)), dma((PARTS, COLS)), dma((PARTS,)), dma((PARTS,)),
            dma((COLS,)), dma((COLS,)), dma((PARTS, COLS)), dma((PARTS, COLS)),
            dma((NG,)), dma((NG,)), dma((NG,)), dma((NG,)),
            dma((NY,)), dma((NY,)), dma((NZ,)), dma((NZ,)),
            dma((NZ,)), dma((NZ,)), dma((NY,)), dma((NY,)),
        ],
        compiler_params=pltpu.CompilerParams(
            collective_id=0, has_side_effects=True, vmem_limit_bytes=VMEM_BYTES
        ),
        name="attend_and_migrate",
    )(page_table, context_len, mig_dest, queries, key_value_scales[0], key_value_pages[0])
    most = count[0, 0]
    choice = sum((most > room).astype(i32) for room in (FIRST,) + ROOM[:-1])
    got_pages = lax.switch(
        choice,
        [lambda packed, crossed, other, pages: pages]
        + [second(room, 1 + i) for i, room in enumerate(ROOM)],
        packed, crossed, other, got_pages,
    )
    return att, got_pages.reshape(1, NG, TOKENS, WIDTH), got_scales[None]


def solution(mesh):
    return jax.shard_map(
        local,
        mesh=mesh,
        in_specs=(
            P(None, "group", "seq"),
            P("group", "seq", None, None),
            P("group", "seq", None),
            P("group", "seq", None),
            P("group"),
            P("group", "seq"),
        ),
        out_specs=(P(None, "group", "seq"), P("group", "seq", None, None), P("group", "seq", None)),
        check_vma=False,
    )
```

time: 136 us -> 109 us (0.80)
  the two profiles are of different devices: /device:TPU:16 before, /device:TPU:33 now
where the time goes in v3:
time: 109 us
  Pallas kernels  103 us (94%)
  local copies, waits for them, and re-layouts  4.35 us (4%)
  between operations  2.36 us (2%)
    pallas_call x1, Pallas kernels, local(): pl.pallas_call(first_kernel, out_shape=(jax.ShapeDtypeStruct(queries.shap...  64.4 us
    pallas_call x1, Pallas kernels, local(): lax.switch(choice, [lambda packed, crossed, other, pages: pages] + [secon...  38.2 us
    unnamed x7, local copies, waits for them, and re-layouts  4.35 us

profile of v3, /device:TPU:33, one launch (start us, length us, event | category | flops | bytes accessed | tf_op | source)
XLA Modules:
  0.0 109.3 jit_solution(1986109962547712524)
XLA Ops:
  0.6 64.4 %attend_and_migrate.1 = (bf16[4,2,256]{2,1,0:T(2,128)(2,1)}, bf16[4,2,2,32,2048]{4,3,2,1,0:T(8,128)(2,1)}, bf16[16,16]{1,0:T(8,128)(2,1)}, bf16[4,64,16,128]{3,2...) custom-call(s32[1,1,16]{2,1,0:T(1,128)} %table_in.1, ...), custom_call_target="tpu_custom_call" | custom-call | tf_op jit(solution)/shard_map/attend_and_migrate/pallas_call | solution.py:505
  66.7 0.0 copy-start.1
  66.7 38.2 %conditional.1 = (bf16[4,2,2,32,2048]{4,3,2,1,0:T(8,128)(2,1)}) conditional(s32[]{:T(128)} %bitcast.2, bf16[4,2,2,32,2048]{4,3,2,1,0:T(8,128)(2,1)} %get-tuple-element.60, (bf16[4,64,16,128]{3,2,1,0:T(8,128)(2,1)}, bf16[4,16,16,128]{3,2,1,0:T(8,128)(2,1)S(1)}, s32[8,1,128]{2,1,0:T(1,128)S(1)}, ...), branch_computations={%region_0.0_spmd, %region_1.0_spmd, %region_2.0_spmd, %region_3.0_... | conditional | bytes 8 | solution.py:570
  66.7 38.2 %cross_25.1 = bf16[4,2,2,32,2048]{4,3,2,1,0:T(8,128)(2,1)} custom-call(bf16[4,64,16,128]{3,2,1,0:T(8,128)(2,1)} %get-tuple-element.36.packed, bf16[4,16,16,128]{3,2,1,0:T(8,128)(2,1)S(1)} %get-tuple-element.37.first_in, s32[8,1,128]{2,1,0:T(1,128)S(1)} %get-tuple-element.38.other_in, ...), custom_call_target="tpu_custom_call", output_to_operand_aliasing={{}: (3, {})} | custom-call | tf_op jit(solution)/shard_map/cond/branch_1_fun/cross_25/pallas_call | solution.py:570
  104.9 0.0 copy-done.1
  104.9 0.6 copy.22
  105.5 0.0 copy-start
  105.5 3.2 %copy.23 = bf16[1,16,32,2048]{3,2,1,0:T(8,128)(2,1)} copy(bf16[1,16,32,2048]{3,2,1,0:T(8,128)(2,1)} %bitcast.6) | data formatting | bytes 4194304
  108.7 0.0 copy-done
  108.7 0.6 copy.24
Async XLA Ops:
  66.7 38.2 %copy-start.1 = (bf16[4,2,256]{2,1,0:T(2,128)(2,1)S(1)}, bf16[4,2,256]{2,1,0:T(2,128)(2,1)}, u32[]{:S(2)}) copy-start(bf16[4,2,256]{2,1,0:T(2,128)(2,1)} %get-tuple-element.74) | copy-start | bytes 12292
  105.5 3.2 %copy-start = (bf16[16,16]{1,0:T(8,128)(2,1)S(1)}, bf16[16,16]{1,0:T(8,128)(2,1)}, u32[]{:S(2)}) copy-start(bf16[16,16]{1,0:T(8,128)(2,1)} %get-tuple-element.64) | copy-start | bytes 1540

commit v4 on v3

--- a/solution.py
+++ b/solution.py
@@ -20,8 +20,10 @@
 STRIPE = WIDTH // COLS
 PARTS, PART_ROWS, PART_COLS = 4, 16, 128
 PAIRS = COLS * COLS
-FIRST = 16
-ROOM = (25, 36, PAIRS)
+UNROLL = 8
+CHUNKS = 8
+FIRST = 25
+ROOM = (36, PAIRS)
 
 
 def part_offsets(p):
@@ -94,7 +96,18 @@
     barrier = pltpu.get_barrier_semaphore()
     for device in devices:
         pl.semaphore_signal(barrier, 1, device_id=device, device_id_type=MESH)
-    pl.semaphore_wait(barrier, len(devices))
+    return lambda: pl.semaphore_wait(barrier, len(devices))
+
+
+def repeat(start, stop, step, carry=0):
+    def steps(i, carry):
+        for k in range(UNROLL):
+            carry = step(start + i * UNROLL + k, carry)
+        return carry
+
+    rounds = (stop - start) // UNROLL
+    carry = lax.fori_loop(0, rounds, steps, carry)
+    return lax.fori_loop(start + rounds * UNROLL, stop, step, carry)
 
 
 def rank_pairs(flags, source_half, dest_half, rank):
@@ -103,7 +116,7 @@
         rank[pair] = jnp.where(present > 0, before, -1)
         return before + present
 
-    lax.fori_loop(0, PAIRS, count_up, jnp.int32(0))
+    repeat(0, PAIRS, count_up, jnp.int32(0))
 
 
 def hand_over(here, p, handed, out_pages, send_sems, recv_sems, own_sem):
@@ -125,7 +138,7 @@
 
 def first_kernel(
     table_in, ctx_in, mig_in, query_in, scales_in, pages_in,
-    att_out, out_pages, scales_out, packed_out, crossed_out, same_out, other_out, count_out,
+    att_out, out_pages, scales_out, packed_out, crossed_out, other_out, choice_out,
     table, ctx, mig, query, scales, pool, half, stripes, packed, handed,
     relay_0, relay_1, relay_2, relay_3, crossed_0, crossed_1, crossed_2, crossed_3,
     qmine, qall, ypart, yland, zpart, zland, scale_rows, sc_send, sc_recv, sc_all,
@@ -149,7 +162,7 @@
     other_peers = [(group_of(here.column_at(d), 1 - zh), s) for d in range(COLS)]
     z_peers = [here.along_z(d) for d in range(1, NZ)]
     y_peers = [here.along_y(d) for d in range(1, NY)]
-    greet(same_peers + other_peers + z_peers + y_peers)
+    all_here = greet(other_peers + z_peers + same_peers + y_peers)
 
     get_mig.wait()
     lane = lax.broadcasted_iota(jnp.int32, (1, DIM), 1)
@@ -159,10 +172,50 @@
             row_flags = jnp.where((lane == mig[r, j]) & (lane != g), 1, row_flags)
     fl_send[...] = row_flags
     fl_same[column] = row_flags
+    get_table.wait()
+
+    def find_pages(i, carry):
+        h = group_of(i % COLS, jnp.where(i < COLS, 1 - zh, zh))
+        here_too, slot = jnp.int32(0), jnp.int32(0)
+        for r in range(RG):
+            for j in range(PPR):
+                hit = mig[r, j] == h
+                slot = jnp.where(hit, table[0, 0, r * PPR + j], slot)
+                here_too = jnp.where(hit, 1, here_too)
+        slots[i] = slot
+        found[i] = jnp.where(h == g, 0, here_too)
+        return carry
+
+    repeat(0, COLS, find_pages)
+    get_pool.wait()
+    for p in range(PARTS):
+        r0, c0 = part_offsets(p)
+
+        def cut_page(b, carry):
+            value = pool[slots[b], r0 : r0 + PART_ROWS]
+            value = jnp.where(found[b] > 0, value, jnp.zeros_like(value))
+            for i in range(COLS):
+                start = i * STRIPE + c0
+                stripes[p, i, b] = value[:, start : start + PART_COLS]
+            return carry
+
+        repeat(0, COLS, cut_page)
+        relays[p][pl.ds(column * COLS, COLS)] = stripes[p, column]
+    all_here()
     same_flags = [
         remote(fl_send, fl_same.at[column], fl_s.at[d], fl_r.at[d], peer)
         for d, peer in enumerate(same_peers, 1)
     ]
+    stripe_copies = []
+    for p in range(PARTS):
+        place = relays[p].at[pl.ds(column * COLS, COLS)]
+        stripe_copies.append(
+            [
+                remote(stripes.at[p, here.column_at(d)], place, st_s.at[p, d], st_r.at[p, d], peer)
+                for d, peer in enumerate(same_peers, 1)
+            ]
+        )
+
     other_flags = [
         remote(fl_send, fl_other.at[column], fl_s.at[COLS + d], fl_r.at[COLS + d], peer)
         for d, peer in enumerate(other_peers)
@@ -183,44 +236,6 @@
         remote(qmine, qall.at[y, zl], zq_s.at[d], zq_r.at[d], peer) for d, peer in enumerate(z_peers, 1)
     ]
 
-    get_table.wait()
-
-    def find_pages(i, carry):
-        h = group_of(i % COLS, jnp.where(i < COLS, 1 - zh, zh))
-        here_too, slot = jnp.int32(0), jnp.int32(0)
-        for r in range(RG):
-            for j in range(PPR):
-                hit = mig[r, j] == h
-                slot = jnp.where(hit, table[0, 0, r * PPR + j], slot)
-                here_too = jnp.where(hit, 1, here_too)
-        slots[i] = slot
-        found[i] = jnp.where(h == g, 0, here_too)
-        return carry
-
-    lax.fori_loop(0, 2 * COLS, find_pages, 0)
-    get_pool.wait()
-    stripe_copies = []
-    for p in range(PARTS):
-        r0, c0 = part_offsets(p)
-
-        def cut_page(b, carry):
-            value = pool[slots[b], r0 : r0 + PART_ROWS]
-            value = jnp.where(found[b] > 0, value, jnp.zeros_like(value))
-            for i in range(COLS):
-                start = i * STRIPE + c0
-                stripes[p, i, b] = value[:, start : start + PART_COLS]
-            return carry
-
-        lax.fori_loop(0, COLS, cut_page, 0)
-        place = relays[p].at[pl.ds(column * COLS, COLS)]
-        stripe_copies.append(
-            [
-                remote(stripes.at[p, here.column_at(d)], place, st_s.at[p, d], st_r.at[p, d], peer)
-                for d, peer in enumerate(same_peers, 1)
-            ]
-        )
-        relays[p][pl.ds(column * COLS, COLS)] = stripes[p, column]
-
     wait(same_flags)
     inside(fl_same, same, out_sem.at[0]).wait()
     following[PAIRS] = PAIRS - 1
@@ -231,21 +246,21 @@
         following[pair] = jnp.where(present > 0, pair, following[pair + 1])
         return carry
 
-    lax.fori_loop(0, PAIRS, look_back, 0)
+    repeat(0, PAIRS, look_back)
 
     def list_pairs(i, cursor):
         pair = following[cursor]
         index[i] = pair
         return jnp.minimum(pair + 1, PAIRS)
 
-    lax.fori_loop(0, PAIRS, list_pairs, jnp.int32(0))
+    cursor = repeat(0, FIRST, list_pairs, jnp.int32(0))
 
     def pack(p, start, stop):
         def step(i, carry):
             packed[p, i] = relays[p][index[i]]
             return carry
 
-        lax.fori_loop(start, stop, step, 0)
+        repeat(start, stop, step)
 
     crossings, y_queries, z_counts = [], [], []
     for p in range(PARTS):
@@ -278,6 +293,7 @@
             ]
     other_copy = inside(fl_other, other, out_sem.at[1])
 
+    repeat(COLS, 2 * COLS, find_pages)
     def half_page(b, carry):
         value = pool[slots[COLS + b]]
         half[b] = jnp.where(found[COLS + b] > 0, value, jnp.zeros_like(value))
@@ -366,6 +382,7 @@
         remote(count, cy.at[y], cy_s.at[d], cy_r.at[d], peer) for d, peer in enumerate(y_peers, 1)
     ]
 
+    repeat(FIRST, PAIRS, list_pairs, cursor)
     for p in range(PARTS):
         pack(p, FIRST, PAIRS)
     outs = [inside(packed, packed_out, out_sem.at[3])]
@@ -396,7 +413,7 @@
             handed[p, pair % COLS, pair // COLS // NC, pair // COLS % NC] = value
             return carry
 
-        lax.fori_loop(0, PAIRS, unpack, 0)
+        repeat(0, PAIRS, unpack)
         handing += hand_over(here, p, handed, out_pages, hd_s, hd_r, own_sem)
         outs.append(inside(crossed[p], crossed_out.at[p], out_sem.at[4 + p]))
 
@@ -422,10 +439,10 @@
     for h in range(NG):
         sc_all[h : h + 1, :] = sc_recv[h]
     scales_out[...] = sc_all[:, : 2 * HEADS].astype(jnp.bfloat16)
-    same_out[...] = fl_same[...]
     other_out[...] = fl_other[...]
     wait(y_counts)
-    count_out[...] = jnp.max(cy[...], axis=0)
+    most = jnp.max(cy[...], axis=0)
+    choice_out[...] = sum((most > room).astype(jnp.int32) for room in (FIRST,) + ROOM[:-1])
     wait(halves)
     wait(outs)
     wait(handing)
@@ -442,7 +459,7 @@
     get_other = inside(other_in, other, in_sem.at[0])
     get_first = inside(first_in, first, in_sem.at[1])
     partner = (group_of(here.column, 1 - here.zh), here.s)
-    greet([partner] + [(group_of(here.column_at(d), here.zh), here.s) for d in range(1, COLS)])
+    greet([partner] + [(group_of(here.column_at(d), here.zh), here.s) for d in range(1, COLS)])()
     crossings = [
         remote(packed.at[p, pl.ds(FIRST, room - FIRST)], rest[p], cr_s.at[p], cr_r.at[p], partner)
         for p in range(PARTS)
@@ -463,9 +480,24 @@
             handed[p, pair % COLS, pair // COLS // NC, pair // COLS % NC] = value
             return carry
 
-        lax.fori_loop(0, PAIRS, unpack, 0)
+        repeat(0, PAIRS, unpack)
         handing += hand_over(here, p, handed, out_pages, hd_s, hd_r, own_sem)
     wait(handing)
+
+
+def last_kernel(att, pages, scales, att_out, pages_out, scales_out, held, att_held, scales_held, sems, out_sems):
+    rows = NG // CHUNKS
+    moves = [
+        (pages.at[pl.ds(i * rows, rows)], held.at[pl.ds(i * rows, rows)], pages_out.at[0, pl.ds(i * rows, rows)])
+        for i in range(CHUNKS)
+    ]
+    moves += [(att, att_held, att_out), (scales, scales_held, scales_out.at[0])]
+    reads = [inside(a, b, sems.at[i]) for i, (a, b, _) in enumerate(moves)]
+    writes = []
+    for i, (_, b, c) in enumerate(moves):
+        reads[i].wait()
+        writes.append(inside(b, c, out_sems.at[i]))
+    wait(writes)
 
 
 dma = pltpu.SemaphoreType.DMA
@@ -502,7 +534,7 @@
 
 
 def local(queries, key_value_pages, key_value_scales, page_table, context_len, mig_dest):
-    att, got_pages, got_scales, packed, crossed, same, other, count = pl.pallas_call(
+    att, got_pages, got_scales, packed, crossed, other, choice = pl.pallas_call(
         first_kernel,
         out_shape=(
             jax.ShapeDtypeStruct(queries.shape, bf16),
@@ -511,11 +543,10 @@
             jax.ShapeDtypeStruct((PARTS, PAIRS) + PART, bf16),
             jax.ShapeDtypeStruct((PARTS, FIRST) + PART, bf16),
             jax.ShapeDtypeStruct((COLS, 1, DIM), i32),
-            jax.ShapeDtypeStruct((COLS, 1, DIM), i32),
-            jax.ShapeDtypeStruct((1, DIM), f32),
+            jax.ShapeDtypeStruct((1, DIM), i32),
         ),
         in_specs=[hbm] * 6,
-        out_specs=(vmem, hbm, vmem, hbm, hbm, vmem, vmem, vmem),
+        out_specs=(vmem, hbm, vmem, hbm, hbm, vmem, vmem),
         scratch_shapes=[
             pltpu.SMEM(page_table.shape, i32),
             pltpu.SMEM(context_len.shape, i32),
@@ -565,15 +596,30 @@
         ),
         name="attend_and_migrate",
     )(page_table, context_len, mig_dest, queries, key_value_scales[0], key_value_pages[0])
-    most = count[0, 0]
-    choice = sum((most > room).astype(i32) for room in (FIRST,) + ROOM[:-1])
     got_pages = lax.switch(
-        choice,
+        choice[0, 0],
         [lambda packed, crossed, other, pages: pages]
         + [second(room, 1 + i) for i, room in enumerate(ROOM)],
         packed, crossed, other, got_pages,
     )
-    return att, got_pages.reshape(1, NG, TOKENS, WIDTH), got_scales[None]
+    return pl.pallas_call(
+        last_kernel,
+        out_shape=(
+            jax.ShapeDtypeStruct(att.shape, bf16),
+            jax.ShapeDtypeStruct((1, NG, TOKENS, WIDTH), bf16),
+            jax.ShapeDtypeStruct((1,) + got_scales.shape, bf16),
+        ),
+        in_specs=[hbm] * 3,
+        out_specs=(hbm,) * 3,
+        scratch_shapes=[
+            pltpu.VMEM((NG, TOKENS, WIDTH), bf16),
+            pltpu.VMEM(att.shape, bf16),
+            pltpu.VMEM(got_scales.shape, bf16),
+            dma((CHUNKS + 2,)), dma((CHUNKS + 2,)),
+        ],
+        compiler_params=pltpu.CompilerParams(vmem_limit_bytes=VMEM_BYTES),
+        name="write_results",
+    )(att, got_pages.reshape(NG, TOKENS, WIDTH), got_scales)
 
 
 def solution(mesh):

time: 109 us -> 74.5 us (0.68)
  the two profiles are of different devices: /device:TPU:33 before, /device:TPU:53 now
where the time goes in v4:
time: 74.5 us; the launch traced here: 74.3 us
  Pallas kernels  73 us (98%)
  between operations  1.32 us (2%)
    pallas_call x1, Pallas kernels, local(): pl.pallas_call(first_kernel, out_shape=(jax.ShapeDtypeStruct(queries.shap...  70.5 us
    pallas_call x1, Pallas kernels, local(): pl.pallas_call(last_kernel, out_shape=(jax.ShapeDtypeStruct(att.shape, bf...  2.43 us

profile of v4, /device:TPU:53, one launch (start us, length us, event | category | flops | bytes accessed | tf_op | source)
XLA Modules:
  0.0 74.3 jit_solution(12075371644971875870)
XLA Ops:
  0.6 70.5 %attend_and_migrate.1 = (bf16[4,2,256]{2,1,0:T(2,128)(2,1)}, bf16[4,2,2,32,2048]{4,3,2,1,0:T(8,128)(2,1)}, bf16[16,16]{1,0:T(8,128)(2,1)}, bf16[4,64,16,128]{3,2...) custom-call(s32[1,1,16]{2,1,0:T(1,128)} %table_in.1, ...), custom_call_target="tpu_custom_call" | custom-call | tf_op jit(solution)/shard_map/attend_and_migrate/pallas_call | solution.py:537
  71.8 2.4 %write_results.1 = (bf16[4,2,256]{2,1,0:T(2,128)(2,1)}, bf16[1,16,32,2048]{3,2,1,0:T(8,128)(2,1)}, bf16[1,16,16]{2,1,0:T(8,128)(2,1)}) custom-call(bf16[4,2,256]{2,1,0:T(2,128)(2,1)} %get-tuple-element.45.att, bf16[16,32,2048]{2,1,0:T(8,128)(2,1)} %bitcast.5, bf16[16,16]{1,0:T(8,128)(2,1)} %get-tuple-element.51.scales), custom_call_target="tpu_custom_call" | custom-call | tf_op jit(solution)/shard_map/write_results/pallas_call | solution.py:605
  (1 shorter events, 0.0 us)

commit v5 on v4

--- a/solution.py
+++ b/solution.py
@@ -141,12 +141,12 @@
     att_out, out_pages, scales_out, packed_out, crossed_out, other_out, choice_out,
     table, ctx, mig, query, scales, pool, half, stripes, packed, handed,
     relay_0, relay_1, relay_2, relay_3, crossed_0, crossed_1, crossed_2, crossed_3,
-    qmine, qall, ypart, yland, zpart, zland, scale_rows, sc_send, sc_recv, sc_all,
+    qmine, qall, ypart, yland, zpart, zland, zlevel, zlevel_land, scale_rows, sc_send, sc_recv, sc_all,
     fl_send, fl_same, fl_other, same, other, cz, cy, count,
     slots, found, following, index, rank,
     in_sem, out_sem, own_sem,
     zq_s, zq_r, yq_s, yq_r, st_s, st_r, cr_s, cr_r, ha_s, ha_r, hd_s, hd_r,
-    sc_s, sc_r, fl_s, fl_r, yr_s, yr_r, zr_s, zr_r, cz_s, cz_r, cy_s, cy_r,
+    sc_s, sc_r, fl_s, fl_r, yr_s, yr_r, zr_s, zr_r, zv_s, zv_r, cz_s, cz_r, cy_s, cy_r,
 ):
     relays = (relay_0, relay_1, relay_2, relay_3)
     crossed = (crossed_0, crossed_1, crossed_2, crossed_3)
@@ -270,12 +270,32 @@
             remote(packed.at[p, pl.ds(0, FIRST)], crossed[p], cr_s.at[p], cr_r.at[p], other_peers[0])
         )
         if p == 0:
+            get_scales.wait()
+            slot_iota = lax.broadcasted_iota(jnp.int32, (NG, SLOTS), 1)
+            dest_iota = lax.broadcasted_iota(jnp.int32, (NG, SLOTS), 0)
+            chosen = jnp.zeros((NG, SLOTS), jnp.float32)
+            for r in range(RG):
+                for j in range(PPR):
+                    chosen = jnp.where(
+                        (dest_iota == mig[r, j]) & (slot_iota == table[0, 0, r * PPR + j]) & (dest_iota != g),
+                        1.0, chosen,
+                    )
+            own_scales = scales[...]
+            rows = jnp.dot(chosen.astype(jnp.bfloat16), own_scales, preferred_element_type=jnp.float32)
+            rows = jnp.concatenate([rows, jnp.zeros((NG, DIM - 2 * HEADS), jnp.float32)], axis=1)
+            for h in range(NG):
+                sc_send[h] = rows[h : h + 1]
+            sc_recv[g] = jnp.zeros((1, DIM), jnp.float32)
+            scale_copies = [
+                remote(sc_send.at[peer[0]], sc_recv.at[g], sc_s.at[d], sc_r.at[d], peer)
+                for d, peer in enumerate(other_peers + same_peers)
+            ]
             wait(z_queries)
             y_queries = [
                 remote(qall.at[y], qall.at[y], yq_s.at[d], yq_r.at[d], peer)
                 for d, peer in enumerate(y_peers, 1)
             ]
-        if p == 1:
+        if p == 0:
             wait(other_flags)
             source = lax.broadcasted_iota(jnp.int32, (COLS, 1, DIM), 2)
             dest_half = (source // NC) % NH
@@ -307,11 +327,7 @@
     ]
     halves.append(inside(half.at[column], own_place, out_sem.at[2]))
 
-    get_scales.wait()
     get_ctx.wait()
-    slot_iota = lax.broadcasted_iota(jnp.int32, (NG, SLOTS), 1)
-    dest_iota = lax.broadcasted_iota(jnp.int32, (NG, SLOTS), 0)
-    chosen = jnp.zeros((NG, SLOTS), jnp.float32)
     token = lax.broadcasted_iota(jnp.int32, (8, LOCAL), 1)
     token_slot, token_in = token // TOKENS, token % TOKENS
     position = jnp.zeros((8, LOCAL), jnp.int32)
@@ -319,22 +335,9 @@
     for r in range(RG):
         for j in range(PPR):
             slot = table[0, 0, r * PPR + j]
-            chosen = jnp.where(
-                (dest_iota == mig[r, j]) & (slot_iota == slot) & (dest_iota != g), 1.0, chosen
-            )
             hit = token_slot == slot
             position = jnp.where(hit, (j * NZ * NY + s) * TOKENS + token_in, position)
             owner = jnp.where(hit, r, owner)
-    own_scales = scales[...]
-    rows = jnp.dot(chosen.astype(jnp.bfloat16), own_scales, preferred_element_type=jnp.float32)
-    rows = jnp.concatenate([rows, jnp.zeros((NG, DIM - 2 * HEADS), jnp.float32)], axis=1)
-    for h in range(NG):
-        sc_send[h] = rows[h : h + 1]
-    sc_recv[g] = jnp.zeros((1, DIM), jnp.float32)
-    scale_copies = [
-        remote(sc_send.at[peer[0]], sc_recv.at[g], sc_s.at[d], sc_r.at[d], peer)
-        for d, peer in enumerate(other_peers + same_peers)
-    ]
     spread = (
         lax.broadcasted_iota(jnp.int32, (SLOTS, LOCAL), 1) // TOKENS
         == lax.broadcasted_iota(jnp.int32, (SLOTS, LOCAL), 0)
@@ -387,18 +390,24 @@
         pack(p, FIRST, PAIRS)
     outs = [inside(packed, packed_out, out_sem.at[3])]
 
+    diagonal = lax.broadcasted_iota(jnp.int32, (ROWS, DIM), 0) == lax.broadcasted_iota(jnp.int32, (ROWS, DIM), 1)
     wait(y_parts)
     terms = yland[:, HEADS].astype(jnp.float32)
     for k in range(HEADS):
         level = sum(terms[:, :, k + i * HEADS : k + i * HEADS + 1] for i in range(3))
         context, level = join(yland[:, k], level)
-        zpart[k, 0] = context.astype(jnp.bfloat16)
-        zpart[k, 1] = with_lanes(jnp.zeros((ROWS, DIM), jnp.float32), 0, 1, level).astype(jnp.bfloat16)
+        zpart[k] = context.astype(jnp.bfloat16)
+        zlevel[k] = jnp.sum(jnp.where(diagonal, level, 0.0), axis=0, keepdims=True)
     z_parts = [
         remote(zpart.at[lax.rem(zl + d, NZ)], zland.at[zl], zr_s.at[d], zr_r.at[d], peer)
         for d, peer in enumerate(z_peers, 1)
     ]
+    z_parts += [
+        remote(zlevel.at[lax.rem(zl + d, NZ)], zlevel_land.at[zl], zv_s.at[d], zv_r.at[d], peer)
+        for d, peer in enumerate(z_peers, 1)
+    ]
     zland[zl] = zpart[zl]
+    zlevel_land[zl] = zlevel[zl]
 
     other_copy.wait()
     rank_pairs(other, 1 - zh, zh, rank)
@@ -418,8 +427,8 @@
         outs.append(inside(crossed[p], crossed_out.at[p], out_sem.at[4 + p]))
 
     wait(z_parts)
-    terms = zland[:, 1].astype(jnp.float32)
-    context, _ = join(zland[:, 0], sum(terms[:, :, i : i + 1] for i in range(3)))
+    levels = jnp.sum(jnp.where(diagonal[None], zlevel_land[...], 0.0), axis=2, keepdims=True)
+    context, _ = join(zland[...], levels)
     for t in range(STEPS):
         att_out[t] = jnp.concatenate(
             [
@@ -564,8 +573,10 @@
             pltpu.VMEM((NY, NZ, ROWS, DIM), bf16),
             pltpu.VMEM((NY, HEADS + 1, ROWS, DIM), bf16),
             pltpu.VMEM((NY, HEADS + 1, ROWS, DIM), bf16),
-            pltpu.VMEM((NZ, 2, ROWS, DIM), bf16),
-            pltpu.VMEM((NZ, 2, ROWS, DIM), bf16),
+            pltpu.VMEM((NZ, ROWS, DIM), bf16),
+            pltpu.VMEM((NZ, ROWS, DIM), bf16),
+            pltpu.VMEM((NZ, 1, DIM), f32),
+            pltpu.VMEM((NZ, 1, DIM), f32),
             pltpu.VMEM((2 * HEADS, LOCAL), f32),
             pltpu.VMEM((NG, 1, DIM), f32),
             pltpu.VMEM((NG, 1, DIM), f32),
@@ -588,7 +599,7 @@
             dma((PARTS, COLS)), dma((PARTS, COLS)), dma((PARTS,)), dma((PARTS,)),
             dma((COLS,)), dma((COLS,)), dma((PARTS, COLS)), dma((PARTS, COLS)),
             dma((NG,)), dma((NG,)), dma((NG,)), dma((NG,)),
-            dma((NY,)), dma((NY,)), dma((NZ,)), dma((NZ,)),
+            dma((NY,)), dma((NY,)), dma((NZ,)), dma((NZ,)), dma((NZ,)), dma((NZ,)),
             dma((NZ,)), dma((NZ,)), dma((NY,)), dma((NY,)),
         ],
         compiler_params=pltpu.CompilerParams(

time: 74.5 us -> 73.9 us (level)
  the two profiles are of different devices: /device:TPU:53 before, /device:TPU:1 now
where the time goes in v5:
time: 73.9 us; the launch traced here: 72.5 us
  Pallas kernels  71.1 us (96%)
  between operations  1.32 us (2%)
    pallas_call x1, Pallas kernels, local(): pl.pallas_call(first_kernel, out_shape=(jax.ShapeDtypeStruct(queries.shap...  68.7 us
    pallas_call x1, Pallas kernels, local(): pl.pallas_call(last_kernel, out_shape=(jax.ShapeDtypeStruct(att.shape, bf...  2.43 us

profile of v5, /device:TPU:1, one launch (start us, length us, event | category | flops | bytes accessed | tf_op | source)
XLA Modules:
  0.0 72.5 jit_solution(7133292335232851003)
XLA Ops:
  0.6 68.7 %attend_and_migrate.1 = (bf16[4,2,256]{2,1,0:T(2,128)(2,1)}, bf16[4,2,2,32,2048]{4,3,2,1,0:T(8,128)(2,1)}, bf16[16,16]{1,0:T(8,128)(2,1)}, bf16[4,64,16,128]{3,2...) custom-call(s32[1,1,16]{2,1,0:T(1,128)} %table_in.1, ...), custom_call_target="tpu_custom_call" | custom-call | tf_op jit(solution)/shard_map/attend_and_migrate/pallas_call | solution.py:546
  70.0 2.4 %write_results.1 = (bf16[4,2,256]{2,1,0:T(2,128)(2,1)}, bf16[1,16,32,2048]{3,2,1,0:T(8,128)(2,1)}, bf16[1,16,16]{2,1,0:T(8,128)(2,1)}) custom-call(bf16[4,2,256]{2,1,0:T(2,128)(2,1)} %get-tuple-element.45.att, bf16[16,32,2048]{2,1,0:T(8,128)(2,1)} %bitcast.5, bf16[16,16]{1,0:T(8,128)(2,1)} %get-tuple-element.51.scales), custom_call_target="tpu_custom_call" | custom-call | tf_op jit(solution)/shard_map/write_results/pallas_call | solution.py:616
  (1 shorter events, 0.0 us)
